TPU v7x, 128 devices: a whole 4x4x4 slice. The times are simulated.
128 devices in a mesh: xb: 16 (over x, y_hi, core), yb: 8 (over y_lo, z).
Axes of the slice: x: 4, y: 4 (y_hi: 2, y_lo: 2; y = y_hi * 2 + y_lo), z: 4, core: 2. Of those that a mesh axis runs over, the one named last changes fastest.
Arguments:
- rhs_coarse: float32 [512, 256, 128], P('xb', 'yb'), may hold values from -1.5 to 1.5
- beta_coarse: float32 [512, 256, 128], P('xb', 'yb'), may hold values from 0.25 to 4
- rhs_mid: float32 [16, 8, 32, 1024], P('xb', 'yb'), may hold values from -6 to 6
- beta_mid: float32 [16, 8, 32, 1024], P('xb', 'yb'), may hold values from 0.25 to 4
- rhs_fine: float32 [16, 8, 2, 32, 1024], P('xb', 'yb'), may hold values from -24 to 24
- beta_fine: float32 [16, 8, 2, 32, 1024], P('xb', 'yb'), may hold values from 0.25 to 4
- parent_mid: int32 [16, 8], replicated, may hold values from 0 to 15, as said below
- offset_mid: int32 [16, 8, 3], replicated, may hold values from 1 to 15
- parent_fine: int32 [16, 8, 2], replicated, may hold values from -1 to 15, as said below
- offset_fine: int32 [16, 8, 2, 3], replicated, may hold values from 1 to 15
Outputs:
- corr_coarse: float32 [512, 256, 128], P('xb', 'yb')
- corr_mid: float32 [16, 8, 32, 1024], P('xb', 'yb')
- corr_fine: float32 [16, 8, 2, 32, 1024], P('xb', 'yb')
Inputs may be any that keep to these rules, and one draw needn't show every extreme that they name: For every j, parent_mid[:, j] is a permutation of 0 to 16 - 1. For every j, each of 0 to 16 - 1 stands in exactly one slot of parent_fine[:, j, :], the other slots are -1, and some device of each column has both slots live.
All inputs are finite; a program needn't handle non-finite values.
Results may differ from a plain program's by a relative error of at most 0.00002.
Values sent between devices are 32-bit elements; how exact they have to be, the bound alone decides.
A program may use at most 64 MiB of HBM per device.

v0:
```python
import functools

import jax
import jax.numpy as jnp
from jax import lax
from jax.experimental import pallas as pl
from jax.experimental.pallas import tpu as pltpu
from jax.sharding import PartitionSpec as P

MESH = pl.DeviceIdType.MESH
F32 = jnp.float32
BF16 = jnp.bfloat16
CH = 64
PAIRS = 20
ROWS = 48
EDGE = 56
WIDE = 2 * EDGE + PAIRS * ROWS
PEERS = [
    (dx, dh, dc)
    for dx, dh in ((2, 1), (1, 1), (3, 1), (2, 0), (0, 1), (1, 0), (3, 0))
    for dc in (0, 1)
] + [(0, 0, 1)]


def iota(shape, dim):
    return lax.broadcasted_iota(jnp.int32, shape, dim)


def each(count, body, unroll=True):
    def step(i, carry):
        body(i)
        return carry

    lax.fori_loop(0, count, step, 0, unroll=unroll)


def chosen_dot(values, choice):
    rows = values.shape[0]
    high = values.astype(BF16).astype(F32)
    rest = values - high
    middle = rest.astype(BF16).astype(F32)
    terms = jnp.concatenate([high, middle, rest - middle], axis=0).astype(BF16)
    out = lax.dot_general(terms, choice, (((1,), (0,)), ((), ())), preferred_element_type=F32)
    return out[:rows] + out[rows : 2 * rows] + out[2 * rows :]


def onehot(mask, value=1.0):
    return jnp.where(mask, value, 0.0).astype(BF16)


class Level:
    def __init__(self, count, scale, refs):
        self.count, self.scale, self.rows = count, scale, count * 128
        (self.full, self.red, self.black, self.coef, self.g, self.inv, self.hb, self.tot, self.rest) = refs

    def field(self, colour):
        return self.black if colour else self.red

    def near(self, colour, at):
        ref = self.field(1 - colour)
        lane = iota((CH, 128), 1)
        odd = (lane // 32 + lane) % 2 == 1
        own = ref[pl.ds(8 + at, CH)]
        above, below = ref[pl.ds(16 + at, CH)], ref[pl.ds(at, CH)]
        after, before = ref[pl.ds(9 + at, CH)], ref[pl.ds(7 + at, CH)]
        other = jnp.where(odd, below, above) if colour else jnp.where(odd, above, below)
        return (
            own,
            other,
            pltpu.roll(jnp.where(lane >= 32, own, after), 96, 1),
            pltpu.roll(jnp.where(lane < 96, own, before), 32, 1),
            pltpu.roll(own, 127, 1),
            pltpu.roll(own, 1, 1),
        )

    def clear_ends(self):
        for ref in (self.red, self.black):
            ref[pl.ds(0, 8)] = jnp.zeros((8, 128), F32)
            ref[pl.ds(8 + self.rows, 8)] = jnp.zeros((8, 128), F32)

    def unfold(self, load):
        for box in range(self.count):
            for s in range(8):
                self.full[pl.ds(box * 256 + s, 32, stride=8)] = load(box, s)

    def packed(self, full, at):
        lane = iota((CH, 128), 1)
        odd = (lane // 32 + lane) % 2 == 1
        planes = full.reshape(CH // 8, 2, 8, 128)
        low, high = planes[:, 0].reshape(CH, 128), planes[:, 1].reshape(CH, 128)
        return jnp.where(odd, high, low), jnp.where(odd, low, high)

    def set_fields(self):
        def body(i):
            at = i * CH
            red, black = self.packed(self.full[pl.ds(2 * at, 2 * CH)], at)
            self.red[pl.ds(8 + at, CH)] = red
            self.black[pl.ds(8 + at, CH)] = black

        each(self.rows // CH, body)

    def set_weights(self):
        def body(i):
            at = i * CH
            lane, row = iota((CH, 128), 1), iota((CH, 128), 0)
            odd = (lane // 32 + lane) % 2 == 1
            s = row % 8
            pair = ((at + row) // 8) % 16
            z = lane % 32
            inside_y = (jnp.logical_not((s == 7) & (lane >= 96)), jnp.logical_not((s == 0) & (lane < 32)))
            inside_z = (z < 31, z > 0)
            for colour in (0, 1):
                first, last = (odd, jnp.logical_not(odd)) if colour else (jnp.logical_not(odd), odd)
                edge = (first & (pair == 0)) | (last & (pair == 15))
                masks = (None, jnp.logical_not(edge)) + inside_y + inside_z
                own = self.field(colour)[pl.ds(8 + at, CH)]
                near = self.near(colour, at)
                faces = [
                    0.5 * (own + (other if mask is None else jnp.where(mask, other, 0.0)))
                    for other, mask in zip(near, masks)
                ]
                total = faces[0] + faces[1] + faces[2] + faces[3] + faces[4] + faces[5]
                inv = 1.0 / total
                for n in range(6):
                    part = faces[n] * inv
                    self.coef[colour, n, pl.ds(at, CH)] = (
                        part if masks[n] is None else jnp.where(masks[n], part, 0.0)
                    )
                self.inv[colour, pl.ds(at, CH)] = inv * (1.0 / self.scale)
                self.hb[colour, pl.ds(at, CH)] = 0.5 * own * inv
                if colour == 0:
                    self.tot[pl.ds(at, CH)] = self.scale * total

        each(self.rows // CH, body)

    def set_target(self, at, red, black):
        for colour, value in ((0, red), (1, black)):
            self.g[colour, pl.ds(at, CH)] = value * self.inv[colour, pl.ds(at, CH)]

    def fresh(self, colour, at):
        near = self.near(colour, at)
        out = self.g[colour, pl.ds(at, CH)]
        for n in range(6):
            out = out + self.coef[colour, n, pl.ds(at, CH)] * near[n]
        return out

    def half_sweep(self, colour):
        def body(i):
            at = i * CH
            self.field(colour)[pl.ds(8 + at, CH)] = self.fresh(colour, at)

        each(self.rows // CH, body)

    def down(self):
        def first(i):
            at = i * CH
            self.red[pl.ds(8 + at, CH)] = self.g[0, pl.ds(at, CH)]

        each(self.rows // CH, first)
        self.half_sweep(1)
        self.half_sweep(0)
        self.half_sweep(1)

        def left(i):
            at = i * CH
            self.rest[pl.ds(at, CH)] = self.tot[pl.ds(at, CH)] * (
                self.fresh(0, at) - self.red[pl.ds(8 + at, CH)]
            )

        each(self.rows // CH, left)

    def restricted(self, mean):
        parts = []
        for box in range(self.count):
            for h in range(2):
                parts.append(
                    jnp.concatenate(
                        [self.rest[pl.ds(box * 128 + 4 * h + j, 16, stride=8)] for j in range(4)], axis=1
                    )
                )
        return chosen_dot(jnp.concatenate(parts, axis=0), mean)

    def start_up(self, pieces, spread):
        sub, lane = iota((8, 128), 0), iota((8, 128), 1)
        odd = (lane // 32 + lane) % 2 == 1
        even = jnp.logical_not(odd)
        rows_of = lane // 32 == sub % 4
        rows_of_face = (
            ((lane < 16) & (sub == 0))
            | ((lane >= 16) & (lane < 32) & (sub == 7))
            | ((lane >= 32) & (lane < 64) & ((lane % 16) // 2 == sub))
        )

        def tiles(rows):
            return jnp.broadcast_to(rows[:, None, :], (rows.shape[0], 8, 128))

        def halves(first, second):
            return jnp.where((sub < 4)[None], tiles(first), tiles(second))

        for box, piece in enumerate(pieces):
            core = jnp.concatenate(
                [
                    halves(piece[0:16], piece[16:32]),
                    halves(piece[48:49], piece[49:50]),
                    halves(piece[50:51], piece[51:52]),
                ],
                axis=0,
            )
            core = jnp.where(rows_of[None], core, 0.0).reshape(144, 128)
            face = jnp.where(rows_of_face[None], tiles(piece[32:48]), 0.0).reshape(128, 128)
            face = jnp.concatenate([face, jnp.zeros((16, 128), F32)], axis=0)
            grown = chosen_dot(jnp.concatenate([core, face], axis=1), spread)
            inner, border = grown[:128, :128], grown[:128, 128:].reshape(16, 8, 128)
            low, high = grown[128:136, :128], grown[136:144, :128]
            at = box * 128
            self.black[pl.ds(8 + at, 128)] = self.black[pl.ds(8 + at, 128)] + inner
            for colour in (0, 1):
                first, last = (odd, even) if colour else (even, odd)
                ghost = jnp.concatenate(
                    [
                        border[:1] + jnp.where(first, low, 0.0)[None],
                        border[1:15],
                        border[15:] + jnp.where(last, high, 0.0)[None],
                    ],
                    axis=0,
                ).reshape(128, 128)
                self.g[colour, pl.ds(at, 128)] = (
                    self.g[colour, pl.ds(at, 128)] + self.hb[colour, pl.ds(at, 128)] * ghost
                )

    def up(self):
        for colour in (0, 1, 0, 1):
            self.half_sweep(colour)

    def finished(self, at):
        lane = iota((CH, 128), 1)
        odd = (lane // 32 + lane) % 2 == 1
        red, black = self.red[pl.ds(8 + at, CH)], self.black[pl.ds(8 + at, CH)]
        low = jnp.where(odd, black, red).reshape(CH // 8, 1, 8, 128)
        high = jnp.where(odd, red, black).reshape(CH // 8, 1, 8, 128)
        return jnp.concatenate([low, high], axis=1).reshape(2 * CH, 128)


def spread_choice():
    l, n = iota((256, 256), 0), iota((256, 256), 1)
    z, q = n % 32, (n % 128) // 32
    inner = (l < 128) & (n < 128) & ((l // 16) % 2 == q // 2) & (l % 16 == z // 2)
    f = l - 128
    along_y = (f >= 0) & (f < 32) & (q == jnp.where(f < 16, 0, 3)) & (z // 2 == f % 16)
    along_z = (f >= 32) & (f < 64) & (q // 2 == f % 2) & (z == jnp.where(f < 48, 0, 31))
    return onehot(inner | ((n >= 128) & (along_y | along_z)))


def mean_choice():
    k, n = iota((512, 128), 0), iota((512, 128), 1)
    lane = k % 128
    return onehot(n == 32 * (k // 128) + 16 * (lane // 64) + (lane % 32) // 2, 0.125)


def place_choice(corner):
    k, n = iota((256, 1024), 0), iota((256, 1024), 1)
    return onehot(n == (k // 16) * 32 + k % 16 + corner[1] * 32 + corner[2])


def window_choice(corner):
    n = iota((1, 384), 1)
    i = n % 16
    source = jnp.where(n < 256, (n // 16) * 32 + i, -4096)
    source = jnp.where((n >= 256) & (n < 272), i - 32, source)
    source = jnp.where((n >= 272) & (n < 288), i + 512, source)
    source = jnp.where((n >= 288) & (n < 304), i * 32 - 1, source)
    source = jnp.where((n >= 304) & (n < 320), i * 32 + 16, source)
    return onehot(iota((1024, 384), 0) == source + corner[1] * 32 + corner[2])


def placed_lhs(piece):
    return jnp.concatenate([piece[0:16], piece[16:32]], axis=1)


def kernel(
    rhs_c, beta_c, rhs_m, beta_m, rhs_f, beta_f, parent_m, offset_m, parent_f, offset_f,
    out_c, out_m, out_f,
    gather1, gather2, gather3, gather4, rim_out, rim_in,
    mean_ref, spread_ref, place_m, place_c, window_m, window_c,
    put_m, put_c, pad_m, pad_c, wide_m, wide_c, cut_m, cut_c,
    beta_e, g_e, field_e, coef_e, inv_e,
    *rest,
):
    fine_refs, mid_refs = rest[:9], rest[9:18]
    send_sems, recv_sems, rim_send, rim_recv = rest[18:]
    fine = Level(2, 1.0, fine_refs)
    mid = Level(1, 0.25, mid_refs)
    n_x, n_y = lax.axis_size("xb"), lax.axis_size("yb")
    row, col = lax.axis_index("xb"), lax.axis_index("yb")

    def beside(dx, dy):
        return (lax.rem(row + dx + n_x, n_x), lax.rem(col + dy + n_y, n_y))

    def peer(dx, dh, dc):
        x, h, c = row // 4, (row // 2) % 2, row % 2
        return (((x + dx) % 4) * 4 + ((h + dh) % 2) * 2 + (c + dc) % 2, col)

    barrier = pltpu.get_barrier_semaphore()
    greeted = [peer(*hop) for hop in PEERS] + [beside(dx, dy) for dx in (-1, 0, 1) for dy in (-1, 1)]
    for device in greeted:
        pl.semaphore_signal(barrier, inc=1, device_id=device, device_id_type=MESH)

    def send_all(buffer, stage):
        for hop in PEERS:
            pltpu.make_async_remote_copy(
                src_ref=buffer.at[row],
                dst_ref=buffer.at[row],
                send_sem=send_sems.at[stage],
                recv_sem=recv_sems.at[stage],
                device_id=peer(*hop),
                device_id_type=MESH,
            ).start()

    def wait_all(buffer, sem):
        whole = buffer.at[pl.ds(0, len(PEERS))]
        pltpu.make_async_copy(whole, whole, sem).wait()

    def send_rim(turn):
        def copy(source, size, target, device):
            pltpu.make_async_remote_copy(
                src_ref=rim_out.at[turn, pl.ds(source, size)],
                dst_ref=rim_in.at[turn, pl.ds(target, size)],
                send_sem=rim_send.at[turn],
                recv_sem=rim_recv.at[turn],
                device_id=device,
                device_id_type=MESH,
            ).start()

        for side_x in (0, 1):
            for side_y in (0, 1):
                copy(
                    256 + 128 * side_y + 112 * side_x, 16,
                    512 + 16 * (2 * (1 - side_x) + 1 - side_y),
                    beside(2 * side_x - 1, 2 * side_y - 1),
                )
        for side in (0, 1):
            copy(256 + 128 * side, 128, 256 + 128 * (1 - side), beside(0, 2 * side - 1))
        for side in (0, 1):
            copy(128 * side, 128, 128 * (1 - side), beside(2 * side - 1, 0))

    def wait_rim(turn, sem):
        whole = rim_in.at[turn]
        pltpu.make_async_copy(whole, whole, sem.at[turn]).wait()

    def fill_rim(turn, ref):
        tile_row = iota((8, 128), 0)
        for side in (0, 1):
            for colour in (0, 1):
                for d in (0, 1):
                    at = EDGE + ((2, 16)[side] + d) * ROWS + 8
                    rim_out[turn, pl.ds(128 * side + (2 * colour + d) * 32, 32)] = ref[colour, pl.ds(at, 32)]

        def body(k):
            at = EDGE + (k + 2) * ROWS
            red, black = ref[0, pl.ds(at + 8, 8)], ref[1, pl.ds(at + 8, 8)]
            rim_out[turn, pl.ds(256 + k * 8, 8)] = jnp.where(tile_row < 4, red, pltpu.roll(black, 4, 0))
            red, black = ref[0, pl.ds(at + 32, 8)], ref[1, pl.ds(at + 32, 8)]
            rim_out[turn, pl.ds(384 + k * 8, 8)] = jnp.where(tile_row < 4, pltpu.roll(black, 4, 0), red)

        each(16, body)

    def take_rim(turn, ref, inside_x, inside_y):
        def keep(value, *sides):
            for side in sides:
                if side is not None:
                    value = jnp.where(side, value, 0.0)
            return value

        for side in (0, 1):
            for colour in (0, 1):
                for d in (0, 1):
                    at = EDGE + ((0, 18)[side] + d) * ROWS + 8
                    part = rim_in[turn, pl.ds(128 * side + (2 * colour + d) * 32, 32)]
                    ref[colour, pl.ds(at, 32)] = keep(part, inside_x[side])

            def body(k, side=side):
                at = EDGE + (k + 2) * ROWS + 40 * side
                part = keep(rim_in[turn, pl.ds(256 + 128 * side + 8 * k, 8)], inside_y[side])
                ref[0, pl.ds(at, 8)] = part
                ref[1, pl.ds(at, 8)] = pltpu.roll(part, 4, 0)

            each(16, body)
            for other in (0, 1):
                for d in (0, 1):
                    at = EDGE + (18 * side + d) * ROWS + 40 * other
                    part = rim_in[turn, pl.ds(512 + 16 * (2 * side + other) + 8 * d, 8)]
                    part = keep(part, inside_x[side], inside_y[other])
                    ref[0, pl.ds(at, 8)] = part
                    ref[1, pl.ds(at, 8)] = pltpu.roll(part, 4, 0)

    mean_ref[...] = mean_choice()
    fine.clear_ends()
    fine.unfold(lambda box, s: beta_f[0, 0, box, :, 128 * s : 128 * s + 128])
    fine.set_fields()
    fine.set_weights()
    fine.unfold(lambda box, s: rhs_f[0, 0, box, :, 128 * s : 128 * s + 128])

    def fine_target(i):
        at = i * CH
        fine.set_target(at, *fine.packed(fine.full[pl.ds(2 * at, 2 * CH)], at))

    each(fine.rows // CH, fine_target)
    fine.down()
    gather1[row] = fine.restricted(mean_ref[...]).reshape(2, 32, 128)
    pl.semaphore_wait(barrier, len(greeted))
    send_all(gather1, 0)

    def own_beta(k):
        lane, line = iota((32, 128), 1), iota((32, 128), 0)
        odd = (line + lane) % 2 == 1
        low, high = beta_c[2 * k], beta_c[2 * k + 1]
        at = EDGE + (k + 2) * ROWS + 8
        beta_e[0, pl.ds(at, 32)] = jnp.where(odd, high, low)
        beta_e[1, pl.ds(at, 32)] = jnp.where(odd, low, high)

    for colour in (0, 1):
        beta_e[colour, pl.ds(0, EDGE)] = jnp.zeros((EDGE, 128), F32)
        beta_e[colour, pl.ds(WIDE - EDGE, EDGE)] = jnp.zeros((EDGE, 128), F32)
    each(16, own_beta, 4)
    fill_rim(0, beta_e)
    send_rim(0)

    mid.clear_ends()
    mid.unfold(lambda box, s: beta_m[0, 0, :, 128 * s : 128 * s + 128])
    mid.set_fields()
    mid.set_weights()
    mid.unfold(lambda box, s: rhs_m[0, 0, :, 128 * s : 128 * s + 128])

    def find_fine(i, carry):
        index, place, x, y, z = carry
        for slot in range(2):
            hit = parent_f[i, col, slot] == row
            index = jnp.where(hit, i, index)
            place = jnp.where(hit, slot, place)
            x = jnp.where(hit, offset_f[i, col, slot, 0], x)
            y = jnp.where(hit, offset_f[i, col, slot, 1], y)
            z = jnp.where(hit, offset_f[i, col, slot, 2], z)
        return index, place, x, y, z

    def find_mid(i, carry):
        index, x, y, z = carry
        hit = parent_m[i, col] == row
        return (
            jnp.where(hit, i, index),
            jnp.where(hit, offset_m[i, col, 0], x),
            jnp.where(hit, offset_m[i, col, 1], y),
            jnp.where(hit, offset_m[i, col, 2], z),
        )

    zero, one = jnp.int32(0), jnp.int32(1)
    child, child_slot, *corner_m = lax.fori_loop(0, 16, find_fine, (zero, zero, one, one, one))
    guest, *corner_c = lax.fori_loop(0, 16, find_mid, (zero, one, one, one))
    place_m[...] = place_choice(corner_m)
    pad_m[0:16] = jnp.zeros((16, 8, 128), F32)
    pad_m[32:48] = jnp.zeros((16, 8, 128), F32)

    wait_all(gather1, recv_sems.at[0])

    put = chosen_dot(placed_lhs(gather1[child, child_slot]), place_m[...])
    for s in range(8):
        put_m[pl.ds(s, 16, stride=8)] = put[:, 128 * s : 128 * s + 128]
    pad_m[16:32] = put_m[...].reshape(16, 8, 128)

    def shift_m(x):
        cut_m[pl.ds(8 * x, 8)] = pad_m[16 - corner_m[0] + x]

    each(32, shift_m)

    def mid_target(i):
        lane, line = iota((2 * CH, 128), 1), iota((2 * CH, 128), 0)
        x = i * (CH // 4) + line // 8 - corner_m[0]
        y = (line % 8) * 4 + lane // 32 - corner_m[1]
        z = lane % 32 - corner_m[2]
        hit = (x >= 0) & (x < 16) & (y >= 0) & (y < 16) & (z >= 0) & (z < 16)
        full = jnp.where(hit, cut_m[pl.ds(2 * CH * i, 2 * CH)], mid.full[pl.ds(2 * CH * i, 2 * CH)])
        mid.set_target(i * CH, *mid.packed(full, i * CH))

    each(mid.rows // CH, mid_target)
    mid.down()
    gather2[row] = mid.restricted(mean_ref[...])
    send_all(gather2, 1)

    place_c[...] = place_choice(corner_c)
    pad_c[0:16] = jnp.zeros((16, 32, 128), F32)
    pad_c[32:48] = jnp.zeros((16, 32, 128), F32)
    wait_rim(0, rim_recv)
    take_rim(0, beta_e, (row > 0, row < n_x - 1), (col > 0, col < n_y - 1))

    def near_wide(ref, colour, at, rows):
        lane, line = iota((rows, 128), 1), iota((rows, 128), 0)
        odd = (line + lane) % 2 == 1
        own = ref[1 - colour, pl.ds(at, rows)]
        above, below = ref[1 - colour, pl.ds(at + ROWS, rows)], ref[1 - colour, pl.ds(at - ROWS, rows)]
        other = jnp.where(odd, below, above) if colour else jnp.where(odd, above, below)
        after, before = ref[1 - colour, pl.ds(at + 1, rows)], ref[1 - colour, pl.ds(at - 1, rows)]
        return own, other, after, before, pltpu.roll(own, 127, 1), pltpu.roll(own, 1, 1)

    def coarse_weights(k):
        lane = iota((ROWS, 128), 1)
        masks = (None, None, None, None, lane < 127, lane > 0)
        at = EDGE + k * ROWS
        for colour in (0, 1):
            own = beta_e[colour, pl.ds(at, ROWS)]
            near = near_wide(beta_e, colour, at, ROWS)
            faces = [
                0.5 * (own + (other if mask is None else jnp.where(mask, other, 0.0)))
                for other, mask in zip(near, masks)
            ]
            total = faces[0] + faces[1] + faces[2] + faces[3] + faces[4] + faces[5]
            real = own > 0.0
            inv = jnp.where(real, 1.0 / total, 0.0)
            for n in range(6):
                keep = real if masks[n] is None else real & masks[n]
                coef_e[colour, n, pl.ds(k * ROWS, ROWS)] = jnp.where(keep, faces[n] * inv, 0.0)
            inv_e[colour, pl.ds(k * ROWS, ROWS)] = 16.0 * inv

    each(PAIRS, coarse_weights, 1)
    window_c[...] = window_choice(corner_c)
    wait_all(gather2, recv_sems.at[1])

    put = chosen_dot(placed_lhs(gather2[guest]), place_c[...])
    for s in range(8):
        part = put[:, 128 * s : 128 * s + 128]
        for q in range(4):
            put_c[pl.ds(4 * s + q, 16, stride=32)] = part if q == 0 else pltpu.roll(part, 128 - 32 * q, 1)

    pad_c[16:32] = put_c[...].reshape(16, 32, 128)

    def coarse_target(k):
        lane, line = iota((32, 128), 1), iota((32, 128), 0)
        odd = (line + lane) % 2 == 1
        y, z = line - corner_c[1], lane - corner_c[2]
        hit = (y >= 0) & (y < 16) & (z >= 0) & (z < 16)
        planes = []
        for d in (0, 1):
            x = 2 * k + d - corner_c[0]
            planes.append(jnp.where(hit & (x >= 0) & (x < 16), pad_c[16 + x], rhs_c[2 * k + d]))
        at = EDGE + (k + 2) * ROWS + 8
        g_e[0, pl.ds(at, 32)] = jnp.where(odd, planes[1], planes[0])
        g_e[1, pl.ds(at, 32)] = jnp.where(odd, planes[0], planes[1])

    each(16, coarse_target, 4)
    fill_rim(1, g_e)
    send_rim(1)
    wait_rim(1, rim_recv)
    take_rim(1, g_e, (None, None), (None, None))

    def coarse_sweep(colour, first, count, line, rows):
        def body(i):
            k = first + i
            at, here = EDGE + k * ROWS + line, k * ROWS + line
            near = near_wide(field_e, colour, at, rows)
            out = g_e[colour, pl.ds(at, rows)] * inv_e[colour, pl.ds(here, rows)]
            for n in range(6):
                out = out + coef_e[colour, n, pl.ds(here, rows)] * near[n]
            field_e[colour, pl.ds(at, rows)] = out

        each(count, body, 2)

    def coarse_first(k):
        field_e[0, pl.ds(EDGE + k * ROWS, ROWS)] = g_e[0, pl.ds(EDGE + k * ROWS, ROWS)] * inv_e[0, pl.ds(k * ROWS, ROWS)]

    each(PAIRS, coarse_first, 4)
    coarse_sweep(1, 1, 18, 0, ROWS)
    coarse_sweep(0, 1, 18, 0, ROWS)
    coarse_sweep(1, 2, 16, 8, 32)

    def coarse_out(k):
        lane, line = iota((32, 128), 1), iota((32, 128), 0)
        odd = (line + lane) % 2 == 1
        at = EDGE + (k + 2) * ROWS + 8
        red, black = field_e[0, pl.ds(at, 32)], field_e[1, pl.ds(at, 32)]
        low, high = jnp.where(odd, black, red), jnp.where(odd, red, black)
        out_c[2 * k] = low
        out_c[2 * k + 1] = high
        wide_c[1 + 2 * k] = low
        wide_c[2 + 2 * k] = high

    each(16, coarse_out, 4)

    def post_window(buffer, lhs, choice):
        got = chosen_dot(lhs, choice)
        for n in range(3):
            buffer[row, pl.ds(16 * n, 16)] = got[1:17, 128 * n : 128 * n + 128]
        for n, (x, h) in enumerate(((0, 0), (0, 1), (17, 0), (17, 1))):
            buffer[row, pl.ds(48 + n, 1)] = got[x : x + 1, 128 * h : 128 * h + 128]

    def cut_window_c(x):
        cut_c[pl.ds(32 * x, 32)] = wide_c[corner_c[0] + x]

    each(18, cut_window_c)
    lane24 = iota((24, 128), 1)
    blocks = []
    for s in range(8):
        block = None
        for q in range(4):
            part = cut_c[pl.ds(4 * s + q, 24, stride=32)]
            if q == 0:
                block = part
            else:
                block = jnp.where(lane24 // 32 == q, pltpu.roll(part, 32 * q, 1), block)
        blocks.append(block)
    post_window(gather3, jnp.concatenate(blocks, axis=1), window_c[...])
    send_all(gather3, 2)
    spread_ref[...] = spread_choice()
    window_m[...] = window_choice(corner_m)
    wait_all(gather3, recv_sems.at[2])

    mid.start_up([gather3[parent_m[row, col]]], spread_ref[...])
    mid.up()

    def mid_out(i):
        full = mid.finished(CH * i)
        mid.full[pl.ds(2 * CH * i, 2 * CH)] = full
        wide_m[pl.ds(1 + CH // 4 * i, CH // 4)] = full.reshape(CH // 4, 8, 128)

    each(mid.rows // CH, mid_out)

    def cut_window_m(x):
        cut_m[pl.ds(8 * x, 8)] = wide_m[corner_m[0] + x]

    each(18, cut_window_m)
    lhs = jnp.concatenate([cut_m[pl.ds(s, 24, stride=8)] for s in range(8)], axis=1)
    post_window(gather4, lhs, window_m[...])
    send_all(gather4, 3)
    for s in range(8):
        out_m[0, 0, :, 128 * s : 128 * s + 128] = mid.full[pl.ds(s, 32, stride=8)]
    wait_all(gather4, recv_sems.at[3])

    owners = [parent_f[row, col, slot] for slot in range(2)]
    fine.start_up([gather4[jnp.maximum(owner, 0)] for owner in owners], spread_ref[...])
    fine.up()

    def fine_out(i):
        fine.full[pl.ds(2 * CH * i, 2 * CH)] = fine.finished(CH * i)

    each(fine.rows // CH, fine_out)
    for box in range(2):
        for s in range(8):
            part = fine.full[pl.ds(box * 256 + s, 32, stride=8)]
            out_f[0, 0, box, :, 128 * s : 128 * s + 128] = jnp.where(owners[box] >= 0, part, 0.0)

    for stage, buffer in enumerate((gather1, gather2, gather3, gather4)):
        wait_all(buffer, send_sems.at[stage])
    for turn in (0, 1):
        wait_rim(turn, rim_send)


def level_scratch(count):
    rows = count * 128
    return [
        pltpu.VMEM((2 * rows, 128), F32),
        pltpu.VMEM((rows + 16, 128), F32),
        pltpu.VMEM((rows + 16, 128), F32),
        pltpu.VMEM((2, 6, rows, 128), F32),
        pltpu.VMEM((2, rows, 128), F32),
        pltpu.VMEM((2, rows, 128), F32),
        pltpu.VMEM((2, rows, 128), F32),
        pltpu.VMEM((rows, 128), F32),
        pltpu.VMEM((rows, 128), F32),
    ]


def on_device(*args):
    shapes = [args[0].shape, args[2].shape, args[4].shape]
    vmem = pl.BlockSpec(memory_space=pltpu.VMEM)
    smem = pl.BlockSpec(memory_space=pltpu.SMEM)
    call = pl.pallas_call(
        kernel,
        out_shape=[jax.ShapeDtypeStruct(shape, F32) for shape in shapes],
        in_specs=[vmem] * 6 + [smem] * 4,
        out_specs=[vmem] * 3,
        scratch_shapes=[
            pltpu.VMEM((16, 2, 32, 128), F32),
            pltpu.VMEM((16, 32, 128), F32),
            pltpu.VMEM((16, 56, 128), F32),
            pltpu.VMEM((16, 56, 128), F32),
            pltpu.VMEM((2, 512, 128), F32),
            pltpu.VMEM((2, 576, 128), F32),
            pltpu.VMEM((512, 128), BF16),
            pltpu.VMEM((256, 256), BF16),
            pltpu.VMEM((256, 1024), BF16),
            pltpu.VMEM((256, 1024), BF16),
            pltpu.VMEM((1024, 384), BF16),
            pltpu.VMEM((1024, 384), BF16),
            pltpu.VMEM((128, 128), F32),
            pltpu.VMEM((512, 128), F32),
            pltpu.VMEM((48, 8, 128), F32),
            pltpu.VMEM((48, 32, 128), F32),
            pltpu.VMEM((33, 8, 128), F32),
            pltpu.VMEM((33, 32, 128), F32),
            pltpu.VMEM((256, 128), F32),
            pltpu.VMEM((24 * 32, 128), F32),
            pltpu.VMEM((2, WIDE, 128), F32),
            pltpu.VMEM((2, WIDE, 128), F32),
            pltpu.VMEM((2, WIDE, 128), F32),
            pltpu.VMEM((2, 6, PAIRS * ROWS, 128), F32),
            pltpu.VMEM((2, PAIRS * ROWS, 128), F32),
            *level_scratch(2),
            *level_scratch(1),
            pltpu.SemaphoreType.DMA((4,)),
            pltpu.SemaphoreType.DMA((4,)),
            pltpu.SemaphoreType.DMA((2,)),
            pltpu.SemaphoreType.DMA((2,)),
        ],
        compiler_params=pltpu.CompilerParams(
            collective_id=0, has_side_effects=True, vmem_limit_bytes=48 * 2**20
        ),
        name="v_cycle",
    )
    return tuple(call(*args))


def solution(mesh):
    return jax.shard_map(
        on_device,
        mesh=mesh,
        in_specs=(
            P("xb", "yb", None),
            P("xb", "yb", None),
            P("xb", "yb", None, None),
            P("xb", "yb", None, None),
            P("xb", "yb", None, None, None),
            P("xb", "yb", None, None, None),
            P(),
            P(),
            P(),
            P(),
        ),
        out_specs=(P("xb", "yb", None), P("xb", "yb", None, None), P("xb", "yb", None, None, None)),
        check_vma=False,
    )
```

profile of v0, /device:TPU:1, one launch (start us, length us, event | category | flops | bytes accessed | tf_op | source)
XLA Modules:
  0.0 65.3 jit_solution(17572277813780673315)
XLA Ops:
  0.6 0.0 copy-start.6
  0.6 0.0 copy-start.2
  0.7 0.8 %copy.13.parent_m = s32[16,8]{1,0:T(8,128)S(1)} copy(s32[16,8]{0,1:T(8,128)} %param.16) | data formatting | bytes 1024 | tf_op args[6]
  1.5 0.0 copy-done.6
  1.5 0.1 copy.14.offset_m
  1.6 0.8 %copy.15.parent_f = s32[16,8,2]{2,1,0:T(8,128)S(1)} copy(s32[16,8,2]{0,2,1:T(2,128)} %param.18) | data formatting | bytes 2048 | tf_op args[8]
  2.4 0.9 %copy.16.offset_f = s32[16,8,2,3]{3,2,1,0:T(2,128)S(1)} copy(s32[16,8,2,3]{0,2,3,1:T(2,128)} %param.19) | data formatting | bytes 6144 | tf_op args[9]
  3.3 0.0 copy-done.2
  3.4 0.0 copy-start
  3.4 1.0 %copy-done = f32[32,32,128]{2,1,0:T(8,128)S(1)} copy-done((f32[32,32,128]{2,1,0:T(8,128)S(1)}, f32[32,32,128]{2,1,0:T(8,128)}, u32[]{:S(2)}) %copy-start) | copy-done | bytes 524312
  4.4 0.0 copy-start.1
  4.4 1.0 %copy-done.1 = f32[32,32,128]{2,1,0:T(8,128)S(1)} copy-done((f32[32,32,128]{2,1,0:T(8,128)S(1)}, f32[32,32,128]{2,1,0:T(8,128)}, u32[]{:S(2)}) %copy-start.1) | copy-done | bytes 524312
  5.4 0.0 copy-start.3
  5.4 0.9 %copy-done.3 = f32[1,1,2,32,1024]{4,3,2,1,0:T(8,128)S(1)} copy-done((f32[1,1,2,32,1024]{4,3,2,1,0:T(8,128)S(1)}, f32[1,1,2,32,1024]{4,3,2,1,0:T(8,128)}, u32[]{:S(2)}) %copy-start.3) | copy-done | bytes 262168
  6.4 0.0 copy-start.4
  6.4 0.9 %copy-done.4 = f32[1,1,32,1024]{3,2,1,0:T(8,128)S(1)} copy-done((f32[1,1,32,1024]{3,2,1,0:T(8,128)S(1)}, f32[1,1,32,1024]{3,2,1,0:T(8,128)}, u32[]{:S(2)}) %copy-start.4) | copy-done | bytes 131096
  7.3 0.0 copy-start.5
  7.3 0.9 %copy-done.5 = f32[1,1,32,1024]{3,2,1,0:T(8,128)S(1)} copy-done((f32[1,1,32,1024]{3,2,1,0:T(8,128)S(1)}, f32[1,1,32,1024]{3,2,1,0:T(8,128)}, u32[]{:S(2)}) %copy-start.5) | copy-done | bytes 131096
  8.2 54.9 %v_cycle.1 = (f32[32,32,128]{2,1,0:T(8,128)S(1)}, f32[1,1,32,1024]{3,2,1,0:T(8,128)S(1)}, f32[1,1,2,32,1024]{4,3,2,1,0:T(8,128)S(1)}) custom-call(f32[32,32,128]{2,1,0:T(8,128)S(1)} %copy-done, f32[32,32,128]{2,1,0:T(8,128)S(1)} %copy-done.1, f32[1,1,32,1024]{3,2,1,0:T(8,128)S(1)} %copy-done.4, f32[1,1,32,1024]{3,2,1,0:T(8,128)S(1)} %copy-done.5, ...), custom_call_target="tpu_custom_call" | custom-call | tf_op jit(solution)/shard_map/v_cycle/pallas_call | solution.py:716
  63.1 0.8 %copy.20 = f32[32,32,128]{2,1,0:T(8,128)} copy(f32[32,32,128]{2,1,0:T(8,128)S(1)} %get-tuple-element.6) | data formatting | bytes 1048576
  63.9 0.7 %copy.21 = f32[1,1,32,1024]{3,2,1,0:T(8,128)} copy(f32[1,1,32,1024]{3,2,1,0:T(8,128)S(1)} %get-tuple-element.7) | data formatting | bytes 262144
  64.6 0.7 %copy.22 = f32[1,1,2,32,1024]{4,3,2,1,0:T(8,128)} copy(f32[1,1,2,32,1024]{4,3,2,1,0:T(8,128)S(1)} %get-tuple-element.8) | data formatting | bytes 524288
Async XLA Ops:
  0.6 0.8 %copy-start.6 = (s32[16,8,3]{0,1,2:T(8,128)S(1)}, s32[16,8,3]{0,1,2:T(8,128)}, u32[]{:S(2)}) copy-start(s32[16,8,3]{0,1,2:T(8,128)} %param.17) | copy-start | bytes 4612
  0.6 2.7 %copy-start.2 = (f32[1,1,2,32,1024]{4,3,2,1,0:T(8,128)S(1)}, f32[1,1,2,32,1024]{4,3,2,1,0:T(8,128)}, u32[]{:S(2)}) copy-start(f32[1,1,2,32,1024]{4,3,2,1,0:T(8,128)} %rhs_f.1) | copy-start | bytes 786436
  3.4 1.0 %copy-start = (f32[32,32,128]{2,1,0:T(8,128)S(1)}, f32[32,32,128]{2,1,0:T(8,128)}, u32[]{:S(2)}) copy-start(f32[32,32,128]{2,1,0:T(8,128)} %rhs_c.1) | copy-start | bytes 1572868
  4.4 1.0 %copy-start.1 = (f32[32,32,128]{2,1,0:T(8,128)S(1)}, f32[32,32,128]{2,1,0:T(8,128)}, u32[]{:S(2)}) copy-start(f32[32,32,128]{2,1,0:T(8,128)} %beta_c.1) | copy-start | bytes 1572868
  5.4 0.9 %copy-start.3 = (f32[1,1,2,32,1024]{4,3,2,1,0:T(8,128)S(1)}, f32[1,1,2,32,1024]{4,3,2,1,0:T(8,128)}, u32[]{:S(2)}) copy-start(f32[1,1,2,32,1024]{4,3,2,1,0:T(8,128)} %beta_f.1) | copy-start | bytes 786436
  6.4 0.9 %copy-start.4 = (f32[1,1,32,1024]{3,2,1,0:T(8,128)S(1)}, f32[1,1,32,1024]{3,2,1,0:T(8,128)}, u32[]{:S(2)}) copy-start(f32[1,1,32,1024]{3,2,1,0:T(8,128)} %rhs_m.1) | copy-start | bytes 393220
  7.3 0.9 %copy-start.5 = (f32[1,1,32,1024]{3,2,1,0:T(8,128)S(1)}, f32[1,1,32,1024]{3,2,1,0:T(8,128)}, u32[]{:S(2)}) copy-start(f32[1,1,32,1024]{3,2,1,0:T(8,128)} %beta_m.1) | copy-start | bytes 393220
where the time goes:
time: 65.7 us; the launch traced here: 65.3 us
  Pallas kernels  54.9 us (84%)
  local copies, waits for them, and re-layouts  9.68 us (15%)
  between operations  0.68 us (1%)
    pallas_call x1, Pallas kernels, on_device(): return tuple(call(*args))  54.9 us
    unnamed x21, local copies, waits for them, and re-layouts  9.68 us

commit v1 on v0

--- a/solution.py
+++ b/solution.py
@@ -15,11 +15,9 @@
 ROWS = 48
 EDGE = 56
 WIDE = 2 * EDGE + PAIRS * ROWS
-PEERS = [
-    (dx, dh, dc)
-    for dx, dh in ((2, 1), (1, 1), (3, 1), (2, 0), (0, 1), (1, 0), (3, 0))
-    for dc in (0, 1)
-] + [(0, 0, 1)]
+CHIPS = ((2, 1), (1, 1), (3, 1), (2, 0), (0, 1), (1, 0), (3, 0))
+SAME_CORE = [(dx, dh, 0) for dx, dh in CHIPS]
+PEERS = [(dx, dh, dc) for dx, dh in CHIPS for dc in (0, 1)] + [(0, 0, 1)]
 
 
 def iota(shape, dim):
@@ -278,21 +276,48 @@
 
 
 def kernel(
+    far_rhs_c, far_beta_c, far_rhs_m, far_beta_m, far_rhs_f, far_beta_f,
+    far_parent_m, far_offset_m, far_parent_f, far_offset_f,
+    far_out_c, far_out_m, far_out_f,
     rhs_c, beta_c, rhs_m, beta_m, rhs_f, beta_f, parent_m, offset_m, parent_f, offset_f,
-    out_c, out_m, out_f,
-    gather1, gather2, gather3, gather4, rim_out, rim_in,
+    out_m, out_f,
+    gather1, gather2, gather3, gather4, relay_out1, relay_in1, relay_out3, relay_in3, relay_out4, relay_in4,
+    rim_out, rim_in,
     mean_ref, spread_ref, place_m, place_c, window_m, window_c,
     put_m, put_c, pad_m, pad_c, wide_m, wide_c, cut_m, cut_c,
     beta_e, g_e, field_e, coef_e, inv_e,
     *rest,
 ):
     fine_refs, mid_refs = rest[:9], rest[9:18]
-    send_sems, recv_sems, rim_send, rim_recv = rest[18:]
+    send_sems, recv_sems, relay_send, relay_recv, rim_send, rim_recv, load_sems, store_sems = rest[18:]
     fine = Level(2, 1.0, fine_refs)
     mid = Level(1, 0.25, mid_refs)
     n_x, n_y = lax.axis_size("xb"), lax.axis_size("yb")
     row, col = lax.axis_index("xb"), lax.axis_index("yb")
 
+    def load(n, source, target):
+        copy = pltpu.make_async_copy(source, target, load_sems.at[n])
+        copy.start()
+        return copy
+
+    def store(n, source, target):
+        copy = pltpu.make_async_copy(source, target, store_sems.at[n])
+        copy.start()
+        return copy
+
+    load_beta_c = load(3, far_beta_c, beta_c)
+    load_beta_f = load(0, far_beta_f.at[0, 0], beta_f)
+    load_rhs_f = load(1, far_rhs_f.at[0, 0], rhs_f)
+    load_beta_m = load(2, far_beta_m.at[0, 0], beta_m)
+    load_rhs_m = load(4, far_rhs_m.at[0, 0], rhs_m)
+    load_rhs_c = load(5, far_rhs_c, rhs_c)
+    load_tables = (
+        load(6, far_parent_m, parent_m),
+        load(7, far_offset_m, offset_m),
+        load(8, far_parent_f.at[col], parent_f),
+        load(9, far_offset_f.at[col], offset_f),
+    )
+
     def beside(dx, dy):
         return (lax.rem(row + dx + n_x, n_x), lax.rem(col + dy + n_y, n_y))
 
@@ -305,28 +330,50 @@
     for device in greeted:
         pl.semaphore_signal(barrier, inc=1, device_id=device, device_id_type=MESH)
 
-    def send_all(buffer, stage):
-        for hop in PEERS:
+    twin = row + 1 - 2 * (row % 2)
+    chip = row // 2
+
+    def send_all(buffer, stage, place, hops):
+        for hop in hops:
             pltpu.make_async_remote_copy(
-                src_ref=buffer.at[row],
-                dst_ref=buffer.at[row],
+                src_ref=buffer.at[place],
+                dst_ref=buffer.at[place],
                 send_sem=send_sems.at[stage],
                 recv_sem=recv_sems.at[stage],
                 device_id=peer(*hop),
                 device_id_type=MESH,
             ).start()
 
-    def wait_all(buffer, sem):
-        whole = buffer.at[pl.ds(0, len(PEERS))]
+    def wait_all(buffer, sem, hops):
+        whole = buffer.at[pl.ds(0, len(hops))]
         pltpu.make_async_copy(whole, whole, sem).wait()
 
+    def wait_one(buffer, sem):
+        pltpu.make_async_copy(buffer, buffer, sem).wait()
+
+    def relay(n, source, target):
+        pltpu.make_async_remote_copy(
+            src_ref=source,
+            dst_ref=target,
+            send_sem=relay_send.at[n],
+            recv_sem=relay_recv.at[n],
+            device_id=(twin, col),
+            device_id_type=MESH,
+        ).start()
+
+    def own_core(device):
+        return lax.rem(device, 2) == row % 2
+
+    def chip_of(device):
+        return lax.div(device, 2)
+
     def send_rim(turn):
-        def copy(source, size, target, device):
+        def copy(kind, source, size, target, device):
             pltpu.make_async_remote_copy(
                 src_ref=rim_out.at[turn, pl.ds(source, size)],
                 dst_ref=rim_in.at[turn, pl.ds(target, size)],
                 send_sem=rim_send.at[turn],
-                recv_sem=rim_recv.at[turn],
+                recv_sem=rim_recv.at[3 * turn + kind],
                 device_id=device,
                 device_id_type=MESH,
             ).start()
@@ -334,18 +381,17 @@
         for side_x in (0, 1):
             for side_y in (0, 1):
                 copy(
-                    256 + 128 * side_y + 112 * side_x, 16,
+                    2, 256 + 128 * side_y + 112 * side_x, 16,
                     512 + 16 * (2 * (1 - side_x) + 1 - side_y),
                     beside(2 * side_x - 1, 2 * side_y - 1),
                 )
         for side in (0, 1):
-            copy(256 + 128 * side, 128, 256 + 128 * (1 - side), beside(0, 2 * side - 1))
+            copy(1, 256 + 128 * side, 128, 256 + 128 * (1 - side), beside(0, 2 * side - 1))
         for side in (0, 1):
-            copy(128 * side, 128, 128 * (1 - side), beside(2 * side - 1, 0))
-
-    def wait_rim(turn, sem):
-        whole = rim_in.at[turn]
-        pltpu.make_async_copy(whole, whole, sem.at[turn]).wait()
+            copy(0, 128 * side, 128, 128 * (1 - side), beside(2 * side - 1, 0))
+
+    def wait_rim(turn, kind):
+        wait_one(rim_in.at[turn, pl.ds(256 * kind, (256, 256, 64)[kind])], rim_recv.at[3 * turn + kind])
 
     def fill_rim(turn, ref):
         tile_row = iota((8, 128), 0)
@@ -364,27 +410,29 @@
 
         each(16, body)
 
-    def take_rim(turn, ref, inside_x, inside_y):
-        def keep(value, *sides):
-            for side in sides:
-                if side is not None:
-                    value = jnp.where(side, value, 0.0)
-            return value
-
+    def keep(value, *sides):
+        for side in sides:
+            if side is not None:
+                value = jnp.where(side, value, 0.0)
+        return value
+
+    def take_y(turn, ref, inside_y):
+        def body(k):
+            for side in (0, 1):
+                at = EDGE + (k + 2) * ROWS + 40 * side
+                part = keep(rim_in[turn, pl.ds(256 + 128 * side + 8 * k, 8)], inside_y[side])
+                ref[0, pl.ds(at, 8)] = part
+                ref[1, pl.ds(at, 8)] = pltpu.roll(part, 4, 0)
+
+        each(16, body)
+
+    def take_x(turn, ref, inside_x, inside_y):
         for side in (0, 1):
             for colour in (0, 1):
                 for d in (0, 1):
                     at = EDGE + ((0, 18)[side] + d) * ROWS + 8
                     part = rim_in[turn, pl.ds(128 * side + (2 * colour + d) * 32, 32)]
                     ref[colour, pl.ds(at, 32)] = keep(part, inside_x[side])
-
-            def body(k, side=side):
-                at = EDGE + (k + 2) * ROWS + 40 * side
-                part = keep(rim_in[turn, pl.ds(256 + 128 * side + 8 * k, 8)], inside_y[side])
-                ref[0, pl.ds(at, 8)] = part
-                ref[1, pl.ds(at, 8)] = pltpu.roll(part, 4, 0)
-
-            each(16, body)
             for other in (0, 1):
                 for d in (0, 1):
                     at = EDGE + (18 * side + d) * ROWS + 40 * other
@@ -395,20 +443,6 @@
 
     mean_ref[...] = mean_choice()
     fine.clear_ends()
-    fine.unfold(lambda box, s: beta_f[0, 0, box, :, 128 * s : 128 * s + 128])
-    fine.set_fields()
-    fine.set_weights()
-    fine.unfold(lambda box, s: rhs_f[0, 0, box, :, 128 * s : 128 * s + 128])
-
-    def fine_target(i):
-        at = i * CH
-        fine.set_target(at, *fine.packed(fine.full[pl.ds(2 * at, 2 * CH)], at))
-
-    each(fine.rows // CH, fine_target)
-    fine.down()
-    gather1[row] = fine.restricted(mean_ref[...]).reshape(2, 32, 128)
-    pl.semaphore_wait(barrier, len(greeted))
-    send_all(gather1, 0)
 
     def own_beta(k):
         lane, line = iota((32, 128), 1), iota((32, 128), 0)
@@ -421,47 +455,78 @@
     for colour in (0, 1):
         beta_e[colour, pl.ds(0, EDGE)] = jnp.zeros((EDGE, 128), F32)
         beta_e[colour, pl.ds(WIDE - EDGE, EDGE)] = jnp.zeros((EDGE, 128), F32)
+    load_beta_c.wait()
     each(16, own_beta, 4)
     fill_rim(0, beta_e)
+    load_beta_f.wait()
+    fine.unfold(lambda box, s: beta_f[box, :, 128 * s : 128 * s + 128])
+    fine.set_fields()
+    fine.set_weights()
+    load_rhs_f.wait()
+    fine.unfold(lambda box, s: rhs_f[box, :, 128 * s : 128 * s + 128])
+
+    def fine_target(i):
+        at = i * CH
+        fine.set_target(at, *fine.packed(fine.full[pl.ds(2 * at, 2 * CH)], at))
+
+    each(fine.rows // CH, fine_target)
+    pl.semaphore_wait(barrier, len(greeted))
     send_rim(0)
+    fine.down()
+    gather1[chip] = fine.restricted(mean_ref[...]).reshape(2, 32, 128)
+    send_all(gather1, 0, chip, SAME_CORE)
 
     mid.clear_ends()
-    mid.unfold(lambda box, s: beta_m[0, 0, :, 128 * s : 128 * s + 128])
+    load_beta_m.wait()
+    mid.unfold(lambda box, s: beta_m[:, 128 * s : 128 * s + 128])
     mid.set_fields()
     mid.set_weights()
-    mid.unfold(lambda box, s: rhs_m[0, 0, :, 128 * s : 128 * s + 128])
+    load_rhs_m.wait()
+    mid.unfold(lambda box, s: rhs_m[:, 128 * s : 128 * s + 128])
+
+    for copy in load_tables:
+        copy.wait()
 
     def find_fine(i, carry):
-        index, place, x, y, z = carry
+        index, place, x, y, z, twin_index, twin_place = carry
         for slot in range(2):
-            hit = parent_f[i, col, slot] == row
+            twin_hit = parent_f[slot, i] == twin
+            twin_index = jnp.where(twin_hit, i, twin_index)
+            twin_place = jnp.where(twin_hit, slot, twin_place)
+            hit = parent_f[slot, i] == row
             index = jnp.where(hit, i, index)
             place = jnp.where(hit, slot, place)
-            x = jnp.where(hit, offset_f[i, col, slot, 0], x)
-            y = jnp.where(hit, offset_f[i, col, slot, 1], y)
-            z = jnp.where(hit, offset_f[i, col, slot, 2], z)
-        return index, place, x, y, z
+            x = jnp.where(hit, offset_f[0, slot, i], x)
+            y = jnp.where(hit, offset_f[1, slot, i], y)
+            z = jnp.where(hit, offset_f[2, slot, i], z)
+        return index, place, x, y, z, twin_index, twin_place
 
     def find_mid(i, carry):
         index, x, y, z = carry
-        hit = parent_m[i, col] == row
+        hit = parent_m[col, i] == row
         return (
             jnp.where(hit, i, index),
-            jnp.where(hit, offset_m[i, col, 0], x),
-            jnp.where(hit, offset_m[i, col, 1], y),
-            jnp.where(hit, offset_m[i, col, 2], z),
+            jnp.where(hit, offset_m[0, col, i], x),
+            jnp.where(hit, offset_m[1, col, i], y),
+            jnp.where(hit, offset_m[2, col, i], z),
         )
 
     zero, one = jnp.int32(0), jnp.int32(1)
-    child, child_slot, *corner_m = lax.fori_loop(0, 16, find_fine, (zero, zero, one, one, one))
+    child, child_slot, *corner_m, twin_child, twin_slot = lax.fori_loop(
+        0, 16, find_fine, (zero, zero, one, one, one, zero, zero)
+    )
     guest, *corner_c = lax.fori_loop(0, 16, find_mid, (zero, one, one, one))
     place_m[...] = place_choice(corner_m)
     pad_m[0:16] = jnp.zeros((16, 8, 128), F32)
     pad_m[32:48] = jnp.zeros((16, 8, 128), F32)
 
-    wait_all(gather1, recv_sems.at[0])
-
-    put = chosen_dot(placed_lhs(gather1[child, child_slot]), place_m[...])
+    wait_all(gather1, recv_sems.at[0], SAME_CORE)
+    relay_out1[...] = gather1[chip_of(twin_child), twin_slot]
+    relay(0, relay_out1, relay_in1)
+    wait_one(relay_in1, relay_recv.at[0])
+
+    piece = jnp.where(own_core(child), gather1[chip_of(child), child_slot], relay_in1[...])
+    put = chosen_dot(placed_lhs(piece), place_m[...])
     for s in range(8):
         put_m[pl.ds(s, 16, stride=8)] = put[:, 128 * s : 128 * s + 128]
     pad_m[16:32] = put_m[...].reshape(16, 8, 128)
@@ -483,13 +548,16 @@
     each(mid.rows // CH, mid_target)
     mid.down()
     gather2[row] = mid.restricted(mean_ref[...])
-    send_all(gather2, 1)
+    send_all(gather2, 1, row, PEERS)
 
     place_c[...] = place_choice(corner_c)
     pad_c[0:16] = jnp.zeros((16, 32, 128), F32)
     pad_c[32:48] = jnp.zeros((16, 32, 128), F32)
-    wait_rim(0, rim_recv)
-    take_rim(0, beta_e, (row > 0, row < n_x - 1), (col > 0, col < n_y - 1))
+    for kind in (0, 1, 2):
+        wait_rim(0, kind)
+    inside_x, inside_y = (row > 0, row < n_x - 1), (col > 0, col < n_y - 1)
+    take_y(0, beta_e, inside_y)
+    take_x(0, beta_e, inside_x, inside_y)
 
     def near_wide(ref, colour, at, rows):
         lane, line = iota((rows, 128), 1), iota((rows, 128), 0)
@@ -521,7 +589,7 @@
 
     each(PAIRS, coarse_weights, 1)
     window_c[...] = window_choice(corner_c)
-    wait_all(gather2, recv_sems.at[1])
+    wait_all(gather2, recv_sems.at[1], PEERS)
 
     put = chosen_dot(placed_lhs(gather2[guest]), place_c[...])
     for s in range(8):
@@ -530,6 +598,8 @@
             put_c[pl.ds(4 * s + q, 16, stride=32)] = part if q == 0 else pltpu.roll(part, 128 - 32 * q, 1)
 
     pad_c[16:32] = put_c[...].reshape(16, 32, 128)
+
+    load_rhs_c.wait()
 
     def coarse_target(k):
         lane, line = iota((32, 128), 1), iota((32, 128), 0)
@@ -547,10 +617,15 @@
     each(16, coarse_target, 4)
     fill_rim(1, g_e)
     send_rim(1)
-    wait_rim(1, rim_recv)
-    take_rim(1, g_e, (None, None), (None, None))
-
-    def coarse_sweep(colour, first, count, line, rows):
+
+    def coarse_first(first, count, line, rows):
+        def body(i):
+            at, here = EDGE + (first + i) * ROWS + line, (first + i) * ROWS + line
+            field_e[0, pl.ds(at, rows)] = g_e[0, pl.ds(at, rows)] * inv_e[0, pl.ds(here, rows)]
+
+        each(count, body, 4 if count % 4 == 0 else True)
+
+    def coarse_sweep(colour, first, count, line=0, rows=ROWS):
         def body(i):
             k = first + i
             at, here = EDGE + k * ROWS + line, k * ROWS + line
@@ -560,15 +635,27 @@
                 out = out + coef_e[colour, n, pl.ds(here, rows)] * near[n]
             field_e[colour, pl.ds(at, rows)] = out
 
-        each(count, body, 2)
-
-    def coarse_first(k):
-        field_e[0, pl.ds(EDGE + k * ROWS, ROWS)] = g_e[0, pl.ds(EDGE + k * ROWS, ROWS)] * inv_e[0, pl.ds(k * ROWS, ROWS)]
-
-    each(PAIRS, coarse_first, 4)
-    coarse_sweep(1, 1, 18, 0, ROWS)
-    coarse_sweep(0, 1, 18, 0, ROWS)
-    coarse_sweep(1, 2, 16, 8, 32)
+        each(count, body, 2 if count % 2 == 0 else True)
+
+    coarse_first(2, 16, 8, 32)
+    wait_rim(1, 1)
+    take_y(1, g_e, (None, None))
+    coarse_first(2, 16, 0, 8)
+    coarse_first(2, 16, 40, 8)
+    coarse_sweep(1, 3, 14)
+    coarse_sweep(0, 4, 12)
+    coarse_sweep(1, 5, 10, 8, 32)
+    wait_rim(1, 0)
+    wait_rim(1, 2)
+    take_x(1, g_e, (None, None), (None, None))
+    for first in (0, 18):
+        coarse_first(first, 2, 0, ROWS)
+    for first in (1, 17):
+        coarse_sweep(1, first, 2)
+    for first in (1, 16):
+        coarse_sweep(0, first, 3)
+    for first in (2, 15):
+        coarse_sweep(1, first, 3, 8, 32)
 
     def coarse_out(k):
         lane, line = iota((32, 128), 1), iota((32, 128), 0)
@@ -576,19 +663,18 @@
         at = EDGE + (k + 2) * ROWS + 8
         red, black = field_e[0, pl.ds(at, 32)], field_e[1, pl.ds(at, 32)]
         low, high = jnp.where(odd, black, red), jnp.where(odd, red, black)
-        out_c[2 * k] = low
-        out_c[2 * k + 1] = high
         wide_c[1 + 2 * k] = low
         wide_c[2 + 2 * k] = high
 
     each(16, coarse_out, 4)
 
-    def post_window(buffer, lhs, choice):
+    def post_window(buffer, stage, lhs, choice):
         got = chosen_dot(lhs, choice)
         for n in range(3):
-            buffer[row, pl.ds(16 * n, 16)] = got[1:17, 128 * n : 128 * n + 128]
+            buffer[chip, pl.ds(16 * n, 16)] = got[1:17, 128 * n : 128 * n + 128]
         for n, (x, h) in enumerate(((0, 0), (0, 1), (17, 0), (17, 1))):
-            buffer[row, pl.ds(48 + n, 1)] = got[x : x + 1, 128 * h : 128 * h + 128]
+            buffer[chip, pl.ds(48 + n, 1)] = got[x : x + 1, 128 * h : 128 * h + 128]
+        send_all(buffer, stage, chip, SAME_CORE)
 
     def cut_window_c(x):
         cut_c[pl.ds(32 * x, 32)] = wide_c[corner_c[0] + x]
@@ -605,13 +691,18 @@
             else:
                 block = jnp.where(lane24 // 32 == q, pltpu.roll(part, 32 * q, 1), block)
         blocks.append(block)
-    post_window(gather3, jnp.concatenate(blocks, axis=1), window_c[...])
-    send_all(gather3, 2)
+    post_window(gather3, 2, jnp.concatenate(blocks, axis=1), window_c[...])
+    store_c = store(0, wide_c.at[pl.ds(1, 32)], far_out_c)
     spread_ref[...] = spread_choice()
     window_m[...] = window_choice(corner_m)
-    wait_all(gather3, recv_sems.at[2])
-
-    mid.start_up([gather3[parent_m[row, col]]], spread_ref[...])
+    wait_all(gather3, recv_sems.at[2], SAME_CORE)
+    relay_out3[...] = gather3[chip_of(parent_m[col, twin])]
+    relay(1, relay_out3, relay_in3)
+    wait_one(relay_in3, relay_recv.at[1])
+
+    owner_m = parent_m[col, row]
+    piece = jnp.where(own_core(owner_m), gather3[chip_of(owner_m)], relay_in3[...])
+    mid.start_up([piece], spread_ref[...])
     mid.up()
 
     def mid_out(i):
@@ -626,14 +717,22 @@
 
     each(18, cut_window_m)
     lhs = jnp.concatenate([cut_m[pl.ds(s, 24, stride=8)] for s in range(8)], axis=1)
-    post_window(gather4, lhs, window_m[...])
-    send_all(gather4, 3)
+    post_window(gather4, 3, lhs, window_m[...])
     for s in range(8):
-        out_m[0, 0, :, 128 * s : 128 * s + 128] = mid.full[pl.ds(s, 32, stride=8)]
-    wait_all(gather4, recv_sems.at[3])
-
-    owners = [parent_f[row, col, slot] for slot in range(2)]
-    fine.start_up([gather4[jnp.maximum(owner, 0)] for owner in owners], spread_ref[...])
+        out_m[:, 128 * s : 128 * s + 128] = mid.full[pl.ds(s, 32, stride=8)]
+    store_m = store(1, out_m, far_out_m.at[0, 0])
+    wait_all(gather4, recv_sems.at[3], SAME_CORE)
+    for slot in range(2):
+        relay_out4[slot] = gather4[chip_of(jnp.maximum(parent_f[slot, twin], 0))]
+    relay(2, relay_out4, relay_in4)
+    wait_one(relay_in4, relay_recv.at[2])
+
+    owners = [parent_f[slot, row] for slot in range(2)]
+    pieces = []
+    for slot, owner in enumerate(owners):
+        owner = jnp.maximum(owner, 0)
+        pieces.append(jnp.where(own_core(owner), gather4[chip_of(owner)], relay_in4[slot]))
+    fine.start_up(pieces, spread_ref[...])
     fine.up()
 
     def fine_out(i):
@@ -643,12 +742,19 @@
     for box in range(2):
         for s in range(8):
             part = fine.full[pl.ds(box * 256 + s, 32, stride=8)]
-            out_f[0, 0, box, :, 128 * s : 128 * s + 128] = jnp.where(owners[box] >= 0, part, 0.0)
-
-    for stage, buffer in enumerate((gather1, gather2, gather3, gather4)):
-        wait_all(buffer, send_sems.at[stage])
+            out_f[box, :, 128 * s : 128 * s + 128] = jnp.where(owners[box] >= 0, part, 0.0)
+    store_f = store(2, out_f, far_out_f.at[0, 0])
+
+    wait_all(gather1, send_sems.at[0], SAME_CORE)
+    wait_all(gather2, send_sems.at[1], PEERS)
+    wait_all(gather3, send_sems.at[2], SAME_CORE)
+    wait_all(gather4, send_sems.at[3], SAME_CORE)
+    for n, buffer in enumerate((relay_out1, relay_out3, relay_out4)):
+        wait_one(buffer, relay_send.at[n])
     for turn in (0, 1):
-        wait_rim(turn, rim_send)
+        wait_one(rim_in.at[turn], rim_send.at[turn])
+    for copy in (store_c, store_m, store_f):
+        copy.wait()
 
 
 def level_scratch(count):
@@ -666,20 +772,47 @@
     ]
 
 
+def write_out(*refs):
+    sources, targets, sems = refs[:3], refs[3:6], refs[6]
+    copies = [pltpu.make_async_copy(*pair, sems.at[n]) for n, pair in enumerate(zip(sources, targets))]
+    for copy in copies:
+        copy.start()
+    for copy in copies:
+        copy.wait()
+
+
 def on_device(*args):
+    fields, (parent_m, offset_m, parent_f, offset_f) = args[:6], args[6:]
+    tables = (
+        jnp.transpose(parent_m),
+        jnp.transpose(offset_m, (2, 1, 0)),
+        jnp.transpose(parent_f, (1, 2, 0)),
+        jnp.transpose(offset_f, (1, 3, 2, 0)),
+    )
     shapes = [args[0].shape, args[2].shape, args[4].shape]
+    out_shape = [jax.ShapeDtypeStruct(shape, F32) for shape in shapes]
     vmem = pl.BlockSpec(memory_space=pltpu.VMEM)
-    smem = pl.BlockSpec(memory_space=pltpu.SMEM)
+    anywhere = pl.BlockSpec(memory_space=pl.ANY)
     call = pl.pallas_call(
         kernel,
-        out_shape=[jax.ShapeDtypeStruct(shape, F32) for shape in shapes],
-        in_specs=[vmem] * 6 + [smem] * 4,
-        out_specs=[vmem] * 3,
+        out_shape=out_shape,
+        in_specs=[pl.BlockSpec(memory_space=pltpu.HBM)] * 10,
+        out_specs=[anywhere] * 3,
         scratch_shapes=[
-            pltpu.VMEM((16, 2, 32, 128), F32),
+            *[pltpu.VMEM(shape, F32) for shape in ((32, 32, 128),) * 2 + ((32, 1024),) * 2 + ((2, 32, 1024),) * 2],
+            *[pltpu.SMEM(shape, jnp.int32) for shape in (tables[0].shape, tables[1].shape, (2, 16), (3, 2, 16))],
+            pltpu.VMEM((32, 1024), F32),
+            pltpu.VMEM((2, 32, 1024), F32),
+            pltpu.VMEM((8, 2, 32, 128), F32),
             pltpu.VMEM((16, 32, 128), F32),
-            pltpu.VMEM((16, 56, 128), F32),
-            pltpu.VMEM((16, 56, 128), F32),
+            pltpu.VMEM((8, 56, 128), F32),
+            pltpu.VMEM((8, 56, 128), F32),
+            pltpu.VMEM((32, 128), F32),
+            pltpu.VMEM((32, 128), F32),
+            pltpu.VMEM((56, 128), F32),
+            pltpu.VMEM((56, 128), F32),
+            pltpu.VMEM((2, 56, 128), F32),
+            pltpu.VMEM((2, 56, 128), F32),
             pltpu.VMEM((2, 512, 128), F32),
             pltpu.VMEM((2, 576, 128), F32),
             pltpu.VMEM((512, 128), BF16),
@@ -705,15 +838,27 @@
             *level_scratch(1),
             pltpu.SemaphoreType.DMA((4,)),
             pltpu.SemaphoreType.DMA((4,)),
+            pltpu.SemaphoreType.DMA((3,)),
+            pltpu.SemaphoreType.DMA((3,)),
             pltpu.SemaphoreType.DMA((2,)),
-            pltpu.SemaphoreType.DMA((2,)),
+            pltpu.SemaphoreType.DMA((6,)),
+            pltpu.SemaphoreType.DMA((10,)),
+            pltpu.SemaphoreType.DMA((3,)),
         ],
         compiler_params=pltpu.CompilerParams(
-            collective_id=0, has_side_effects=True, vmem_limit_bytes=48 * 2**20
+            collective_id=0, has_side_effects=True, vmem_limit_bytes=60 * 2**20
         ),
         name="v_cycle",
     )
-    return tuple(call(*args))
+    write = pl.pallas_call(
+        write_out,
+        out_shape=out_shape,
+        in_specs=[vmem] * 3,
+        out_specs=[anywhere] * 3,
+        scratch_shapes=[pltpu.SemaphoreType.DMA((3,))],
+        name="write_out",
+    )
+    return tuple(write(*call(*fields, *tables)))
 
 
 def solution(mesh):

time: 65.7 us -> 50.9 us (0.77)
  local copies, waits for them, and re-layouts: 9.68 us -> 0 us
  Pallas kernels: 54.9 us -> 50.1 us
    unnamed x21 -> x0, local copies, waits for them, and re-layouts: 9.68 us -> none
    pallas_call x1 -> x2, Pallas kernels: 54.9 us -> 50.1 us  [on_device(): return tuple(write(*call(*fields, *tables)))]
where the time goes in v1:
time: 50.9 us; the launch traced here: 50.7 us
  Pallas kernels  50.1 us (98%)
  between operations  0.64 us (1%)
    pallas_call x2, Pallas kernels, on_device(): return tuple(write(*call(*fields, *tables)))  50.1 us

profile of v1, /device:TPU:1, one launch (start us, length us, event | category | flops | bytes accessed | tf_op | source)
XLA Modules:
  0.0 50.7 jit_solution(3317952138927607319)
XLA Ops:
  0.6 48.0 %v_cycle.1 = (f32[32,32,128]{2,1,0:T(8,128)}, f32[1,1,32,1024]{3,2,1,0:T(8,128)}, f32[1,1,2,32,1024]{4,3,2,1,0:T(8,128)}) custom-call(f32[32,32,128]{2,1,0:T(8,128)} %far_rhs_c.1, f32[32,32,128]{2,1,0:T(8,128)} %far_beta_c.1, f32[1,1,32,1024]{3,2,1,0:T(8,128)} %far_rhs_m.1, f32[1,1,32,1024]{3,2,1,0:T(8,128)} %far_beta_m.1, f32[1,1,2,32,1024]{4,3,2,1,0:T(8,128)} %far_rhs_f.1, ...), custom_call_target="tpu_custom_call" | custom-call | tf_op jit(solution)/shard_map/v_cycle/pallas_call | solution.py:861
  48.6 2.1 %write_out.1 = (f32[32,32,128]{2,1,0:T(8,128)}, f32[1,1,32,1024]{3,2,1,0:T(8,128)}, f32[1,1,2,32,1024]{4,3,2,1,0:T(8,128)}) custom-call(f32[32,32,128]{2,1,0:T(8,128)} %get-tuple-element.6.refs_0_, f32[1,1,32,1024]{3,2,1,0:T(8,128)} %get-tuple-element.7.refs_1_, f32[1,1,2,32,1024]{4,3,2,1,0:T(8,128)} %get-tuple-element.8.refs_2_), custom_call_target="tpu_custom_call" | custom-call | tf_op jit(solution)/shard_map/write_out/pallas_call | solution.py:861

commit v2 on v1

--- a/solution.py
+++ b/solution.py
@@ -278,9 +278,8 @@
 def kernel(
     far_rhs_c, far_beta_c, far_rhs_m, far_beta_m, far_rhs_f, far_beta_f,
     far_parent_m, far_offset_m, far_parent_f, far_offset_f,
-    far_out_c, far_out_m, far_out_f,
+    out_c, out_m, out_f,
     rhs_c, beta_c, rhs_m, beta_m, rhs_f, beta_f, parent_m, offset_m, parent_f, offset_f,
-    out_m, out_f,
     gather1, gather2, gather3, gather4, relay_out1, relay_in1, relay_out3, relay_in3, relay_out4, relay_in4,
     rim_out, rim_in,
     mean_ref, spread_ref, place_m, place_c, window_m, window_c,
@@ -289,7 +288,7 @@
     *rest,
 ):
     fine_refs, mid_refs = rest[:9], rest[9:18]
-    send_sems, recv_sems, relay_send, relay_recv, rim_send, rim_recv, load_sems, store_sems = rest[18:]
+    send_sems, recv_sems, relay_send, relay_recv, rim_send, rim_recv, load_sems, store_sem = rest[18:]
     fine = Level(2, 1.0, fine_refs)
     mid = Level(1, 0.25, mid_refs)
     n_x, n_y = lax.axis_size("xb"), lax.axis_size("yb")
@@ -297,11 +296,6 @@
 
     def load(n, source, target):
         copy = pltpu.make_async_copy(source, target, load_sems.at[n])
-        copy.start()
-        return copy
-
-    def store(n, source, target):
-        copy = pltpu.make_async_copy(source, target, store_sems.at[n])
         copy.start()
         return copy
 
@@ -456,7 +450,7 @@
         beta_e[colour, pl.ds(0, EDGE)] = jnp.zeros((EDGE, 128), F32)
         beta_e[colour, pl.ds(WIDE - EDGE, EDGE)] = jnp.zeros((EDGE, 128), F32)
     load_beta_c.wait()
-    each(16, own_beta, 4)
+    each(16, own_beta)
     fill_rim(0, beta_e)
     load_beta_f.wait()
     fine.unfold(lambda box, s: beta_f[box, :, 128 * s : 128 * s + 128])
@@ -587,7 +581,7 @@
                 coef_e[colour, n, pl.ds(k * ROWS, ROWS)] = jnp.where(keep, faces[n] * inv, 0.0)
             inv_e[colour, pl.ds(k * ROWS, ROWS)] = 16.0 * inv
 
-    each(PAIRS, coarse_weights, 1)
+    each(PAIRS, coarse_weights, 4)
     window_c[...] = window_choice(corner_c)
     wait_all(gather2, recv_sems.at[1], PEERS)
 
@@ -614,7 +608,7 @@
         g_e[0, pl.ds(at, 32)] = jnp.where(odd, planes[1], planes[0])
         g_e[1, pl.ds(at, 32)] = jnp.where(odd, planes[0], planes[1])
 
-    each(16, coarse_target, 4)
+    each(16, coarse_target)
     fill_rim(1, g_e)
     send_rim(1)
 
@@ -623,7 +617,7 @@
             at, here = EDGE + (first + i) * ROWS + line, (first + i) * ROWS + line
             field_e[0, pl.ds(at, rows)] = g_e[0, pl.ds(at, rows)] * inv_e[0, pl.ds(here, rows)]
 
-        each(count, body, 4 if count % 4 == 0 else True)
+        each(count, body)
 
     def coarse_sweep(colour, first, count, line=0, rows=ROWS):
         def body(i):
@@ -635,7 +629,7 @@
                 out = out + coef_e[colour, n, pl.ds(here, rows)] * near[n]
             field_e[colour, pl.ds(at, rows)] = out
 
-        each(count, body, 2 if count % 2 == 0 else True)
+        each(count, body)
 
     coarse_first(2, 16, 8, 32)
     wait_rim(1, 1)
@@ -666,7 +660,7 @@
         wide_c[1 + 2 * k] = low
         wide_c[2 + 2 * k] = high
 
-    each(16, coarse_out, 4)
+    each(16, coarse_out)
 
     def post_window(buffer, stage, lhs, choice):
         got = chosen_dot(lhs, choice)
@@ -692,7 +686,8 @@
                 block = jnp.where(lane24 // 32 == q, pltpu.roll(part, 32 * q, 1), block)
         blocks.append(block)
     post_window(gather3, 2, jnp.concatenate(blocks, axis=1), window_c[...])
-    store_c = store(0, wide_c.at[pl.ds(1, 32)], far_out_c)
+    store_c = pltpu.make_async_copy(wide_c.at[pl.ds(1, 32)], out_c, store_sem)
+    store_c.start()
     spread_ref[...] = spread_choice()
     window_m[...] = window_choice(corner_m)
     wait_all(gather3, recv_sems.at[2], SAME_CORE)
@@ -719,8 +714,7 @@
     lhs = jnp.concatenate([cut_m[pl.ds(s, 24, stride=8)] for s in range(8)], axis=1)
     post_window(gather4, 3, lhs, window_m[...])
     for s in range(8):
-        out_m[:, 128 * s : 128 * s + 128] = mid.full[pl.ds(s, 32, stride=8)]
-    store_m = store(1, out_m, far_out_m.at[0, 0])
+        out_m[0, 0, :, 128 * s : 128 * s + 128] = mid.full[pl.ds(s, 32, stride=8)]
     wait_all(gather4, recv_sems.at[3], SAME_CORE)
     for slot in range(2):
         relay_out4[slot] = gather4[chip_of(jnp.maximum(parent_f[slot, twin], 0))]
@@ -742,8 +736,7 @@
     for box in range(2):
         for s in range(8):
             part = fine.full[pl.ds(box * 256 + s, 32, stride=8)]
-            out_f[box, :, 128 * s : 128 * s + 128] = jnp.where(owners[box] >= 0, part, 0.0)
-    store_f = store(2, out_f, far_out_f.at[0, 0])
+            out_f[0, 0, box, :, 128 * s : 128 * s + 128] = jnp.where(owners[box] >= 0, part, 0.0)
 
     wait_all(gather1, send_sems.at[0], SAME_CORE)
     wait_all(gather2, send_sems.at[1], PEERS)
@@ -753,8 +746,7 @@
         wait_one(buffer, relay_send.at[n])
     for turn in (0, 1):
         wait_one(rim_in.at[turn], rim_send.at[turn])
-    for copy in (store_c, store_m, store_f):
-        copy.wait()
+    store_c.wait()
 
 
 def level_scratch(count):
@@ -773,8 +765,8 @@
 
 
 def write_out(*refs):
-    sources, targets, sems = refs[:3], refs[3:6], refs[6]
-    copies = [pltpu.make_async_copy(*pair, sems.at[n]) for n, pair in enumerate(zip(sources, targets))]
+    sources, targets, sem = refs[:3], refs[3:6], refs[6]
+    copies = [pltpu.make_async_copy(x, y, sem.at[n]) for n, (x, y) in enumerate(zip(sources, targets))]
     for copy in copies:
         copy.start()
     for copy in copies:
@@ -791,18 +783,15 @@
     )
     shapes = [args[0].shape, args[2].shape, args[4].shape]
     out_shape = [jax.ShapeDtypeStruct(shape, F32) for shape in shapes]
-    vmem = pl.BlockSpec(memory_space=pltpu.VMEM)
     anywhere = pl.BlockSpec(memory_space=pl.ANY)
     call = pl.pallas_call(
         kernel,
         out_shape=out_shape,
         in_specs=[pl.BlockSpec(memory_space=pltpu.HBM)] * 10,
-        out_specs=[anywhere] * 3,
+        out_specs=[pl.BlockSpec(memory_space=pltpu.VMEM)] * 3,
         scratch_shapes=[
             *[pltpu.VMEM(shape, F32) for shape in ((32, 32, 128),) * 2 + ((32, 1024),) * 2 + ((2, 32, 1024),) * 2],
             *[pltpu.SMEM(shape, jnp.int32) for shape in (tables[0].shape, tables[1].shape, (2, 16), (3, 2, 16))],
-            pltpu.VMEM((32, 1024), F32),
-            pltpu.VMEM((2, 32, 1024), F32),
             pltpu.VMEM((8, 2, 32, 128), F32),
             pltpu.VMEM((16, 32, 128), F32),
             pltpu.VMEM((8, 56, 128), F32),
@@ -843,22 +832,24 @@
             pltpu.SemaphoreType.DMA((2,)),
             pltpu.SemaphoreType.DMA((6,)),
             pltpu.SemaphoreType.DMA((10,)),
-            pltpu.SemaphoreType.DMA((3,)),
+            pltpu.SemaphoreType.DMA,
         ],
         compiler_params=pltpu.CompilerParams(
-            collective_id=0, has_side_effects=True, vmem_limit_bytes=60 * 2**20
+            collective_id=0, has_side_effects=True, vmem_limit_bytes=40 * 2**20
         ),
         name="v_cycle",
     )
     write = pl.pallas_call(
         write_out,
         out_shape=out_shape,
-        in_specs=[vmem] * 3,
+        in_specs=[pl.BlockSpec(memory_space=pltpu.VMEM)] * 3,
         out_specs=[anywhere] * 3,
         scratch_shapes=[pltpu.SemaphoreType.DMA((3,))],
+        compiler_params=pltpu.CompilerParams(vmem_limit_bytes=8 * 2**20),
         name="write_out",
     )
-    return tuple(write(*call(*fields, *tables)))
+    pinned = [pltpu.with_memory_space_constraint(arg, pltpu.HBM) for arg in fields + tables]
+    return tuple(write(*call(*pinned)))
 
 
 def solution(mesh):

time: 50.9 us -> 47.5 us (0.933)
  Pallas kernels: 50.1 us -> 46.8 us
    pallas_call x2, Pallas kernels: 50.1 us -> 46.8 us  [on_device(): return tuple(write(*call(*pinned)))]
where the time goes in v2:
time: 47.5 us; the launch traced here: 47.4 us
  Pallas kernels  46.8 us (99%)
  between operations  0.64 us (1%)
    pallas_call x2, Pallas kernels, on_device(): return tuple(write(*call(*pinned)))  46.8 us

profile of v2, /device:TPU:1, one launch (start us, length us, event | category | flops | bytes accessed | tf_op | source)
XLA Modules:
  0.0 47.4 jit_solution(6307068674963691577)
XLA Ops:
  0.6 45.8 %v_cycle.1 = (f32[32,32,128]{2,1,0:T(8,128)S(1)}, f32[1,1,32,1024]{3,2,1,0:T(8,128)S(1)}, f32[1,1,2,32,1024]{4,3,2,1,0:T(8,128)S(1)}) custom-call(f32[32,32,128]{2,1,0:T(8,128)} %far_rhs_c.1, f32[32,32,128]{2,1,0:T(8,128)} %far_beta_c.1, f32[1,1,32,1024]{3,2,1,0:T(8,128)} %far_rhs_m.1, f32[1,1,32,1024]{3,2,1,0:T(8,128)} %far_beta_m.1, ...), custom_call_target="tpu_custom_call" | custom-call | tf_op jit(solution)/shard_map/v_cycle/pallas_call | solution.py:852
  46.5 0.9 %write_out.1 = (f32[32,32,128]{2,1,0:T(8,128)}, f32[1,1,32,1024]{3,2,1,0:T(8,128)}, f32[1,1,2,32,1024]{4,3,2,1,0:T(8,128)}) custom-call(f32[32,32,128]{2,1,0:T(8,128)S(1)} %get-tuple-element.6.refs_0_, f32[1,1,32,1024]{3,2,1,0:T(8,128)S(1)} %get-tuple-element.7.refs_1_, f32[1,1,2,32,1024]{4,3,2,1,0:T(8,128)S(1)} %get-tuple-element.8.refs_2_), custom_call_target="tpu_custom_call" | custom-call | tf_op jit(solution)/shard_map/write_out/pallas_call | solution.py:852

commit v3 on v2

--- a/solution.py
+++ b/solution.py
@@ -280,7 +280,7 @@
     far_parent_m, far_offset_m, far_parent_f, far_offset_f,
     out_c, out_m, out_f,
     rhs_c, beta_c, rhs_m, beta_m, rhs_f, beta_f, parent_m, offset_m, parent_f, offset_f,
-    gather1, gather2, gather3, gather4, relay_out1, relay_in1, relay_out3, relay_in3, relay_out4, relay_in4,
+    gather1, gather2, gather3, gather4, relay_out1, relay_in1, relay_out2, relay_in2, relay_out3, relay_in3, relay_out4, relay_in4,
     rim_out, rim_in,
     mean_ref, spread_ref, place_m, place_c, window_m, window_c,
     put_m, put_c, pad_m, pad_c, wide_m, wide_c, cut_m, cut_c,
@@ -288,7 +288,7 @@
     *rest,
 ):
     fine_refs, mid_refs = rest[:9], rest[9:18]
-    send_sems, recv_sems, relay_send, relay_recv, rim_send, rim_recv, load_sems, store_sem = rest[18:]
+    send_sems, recv_sems, relay_send, relay_recv, rim_send, rim_recv, load_sems = rest[18:]
     fine = Level(2, 1.0, fine_refs)
     mid = Level(1, 0.25, mid_refs)
     n_x, n_y = lax.axis_size("xb"), lax.axis_size("yb")
@@ -299,9 +299,9 @@
         copy.start()
         return copy
 
-    load_beta_c = load(3, far_beta_c, beta_c)
     load_beta_f = load(0, far_beta_f.at[0, 0], beta_f)
     load_rhs_f = load(1, far_rhs_f.at[0, 0], rhs_f)
+    load_beta_c = load(3, far_beta_c, beta_c)
     load_beta_m = load(2, far_beta_m.at[0, 0], beta_m)
     load_rhs_m = load(4, far_rhs_m.at[0, 0], rhs_m)
     load_rhs_c = load(5, far_rhs_c, rhs_c)
@@ -438,6 +438,23 @@
     mean_ref[...] = mean_choice()
     fine.clear_ends()
 
+    load_beta_f.wait()
+    fine.unfold(lambda box, s: beta_f[box, :, 128 * s : 128 * s + 128])
+    fine.set_fields()
+    fine.set_weights()
+    load_rhs_f.wait()
+    fine.unfold(lambda box, s: rhs_f[box, :, 128 * s : 128 * s + 128])
+
+    def fine_target(i):
+        at = i * CH
+        fine.set_target(at, *fine.packed(fine.full[pl.ds(2 * at, 2 * CH)], at))
+
+    each(fine.rows // CH, fine_target)
+    pl.semaphore_wait(barrier, len(greeted))
+    fine.down()
+    gather1[chip] = fine.restricted(mean_ref[...]).reshape(2, 32, 128)
+    send_all(gather1, 0, chip, SAME_CORE)
+
     def own_beta(k):
         lane, line = iota((32, 128), 1), iota((32, 128), 0)
         odd = (line + lane) % 2 == 1
@@ -452,24 +469,7 @@
     load_beta_c.wait()
     each(16, own_beta)
     fill_rim(0, beta_e)
-    load_beta_f.wait()
-    fine.unfold(lambda box, s: beta_f[box, :, 128 * s : 128 * s + 128])
-    fine.set_fields()
-    fine.set_weights()
-    load_rhs_f.wait()
-    fine.unfold(lambda box, s: rhs_f[box, :, 128 * s : 128 * s + 128])
-
-    def fine_target(i):
-        at = i * CH
-        fine.set_target(at, *fine.packed(fine.full[pl.ds(2 * at, 2 * CH)], at))
-
-    each(fine.rows // CH, fine_target)
-    pl.semaphore_wait(barrier, len(greeted))
     send_rim(0)
-    fine.down()
-    gather1[chip] = fine.restricted(mean_ref[...]).reshape(2, 32, 128)
-    send_all(gather1, 0, chip, SAME_CORE)
-
     mid.clear_ends()
     load_beta_m.wait()
     mid.unfold(lambda box, s: beta_m[:, 128 * s : 128 * s + 128])
@@ -496,20 +496,21 @@
         return index, place, x, y, z, twin_index, twin_place
 
     def find_mid(i, carry):
-        index, x, y, z = carry
+        index, x, y, z, twin_index = carry
         hit = parent_m[col, i] == row
         return (
             jnp.where(hit, i, index),
             jnp.where(hit, offset_m[0, col, i], x),
             jnp.where(hit, offset_m[1, col, i], y),
             jnp.where(hit, offset_m[2, col, i], z),
+            jnp.where(parent_m[col, i] == twin, i, twin_index),
         )
 
     zero, one = jnp.int32(0), jnp.int32(1)
     child, child_slot, *corner_m, twin_child, twin_slot = lax.fori_loop(
         0, 16, find_fine, (zero, zero, one, one, one, zero, zero)
     )
-    guest, *corner_c = lax.fori_loop(0, 16, find_mid, (zero, one, one, one))
+    guest, *corner_c, twin_guest = lax.fori_loop(0, 16, find_mid, (zero, one, one, one, zero))
     place_m[...] = place_choice(corner_m)
     pad_m[0:16] = jnp.zeros((16, 8, 128), F32)
     pad_m[32:48] = jnp.zeros((16, 8, 128), F32)
@@ -541,8 +542,8 @@
 
     each(mid.rows // CH, mid_target)
     mid.down()
-    gather2[row] = mid.restricted(mean_ref[...])
-    send_all(gather2, 1, row, PEERS)
+    gather2[chip] = mid.restricted(mean_ref[...])
+    send_all(gather2, 1, chip, SAME_CORE)
 
     place_c[...] = place_choice(corner_c)
     pad_c[0:16] = jnp.zeros((16, 32, 128), F32)
@@ -583,9 +584,13 @@
 
     each(PAIRS, coarse_weights, 4)
     window_c[...] = window_choice(corner_c)
-    wait_all(gather2, recv_sems.at[1], PEERS)
-
-    put = chosen_dot(placed_lhs(gather2[guest]), place_c[...])
+    wait_all(gather2, recv_sems.at[1], SAME_CORE)
+    relay_out2[...] = gather2[chip_of(twin_guest)]
+    relay(3, relay_out2, relay_in2)
+    wait_one(relay_in2, relay_recv.at[3])
+
+    piece = jnp.where(own_core(guest), gather2[chip_of(guest)], relay_in2[...])
+    put = chosen_dot(placed_lhs(piece), place_c[...])
     for s in range(8):
         part = put[:, 128 * s : 128 * s + 128]
         for q in range(4):
@@ -686,8 +691,7 @@
                 block = jnp.where(lane24 // 32 == q, pltpu.roll(part, 32 * q, 1), block)
         blocks.append(block)
     post_window(gather3, 2, jnp.concatenate(blocks, axis=1), window_c[...])
-    store_c = pltpu.make_async_copy(wide_c.at[pl.ds(1, 32)], out_c, store_sem)
-    store_c.start()
+    out_c[...] = wide_c[1:33]
     spread_ref[...] = spread_choice()
     window_m[...] = window_choice(corner_m)
     wait_all(gather3, recv_sems.at[2], SAME_CORE)
@@ -739,14 +743,13 @@
             out_f[0, 0, box, :, 128 * s : 128 * s + 128] = jnp.where(owners[box] >= 0, part, 0.0)
 
     wait_all(gather1, send_sems.at[0], SAME_CORE)
-    wait_all(gather2, send_sems.at[1], PEERS)
+    wait_all(gather2, send_sems.at[1], SAME_CORE)
     wait_all(gather3, send_sems.at[2], SAME_CORE)
     wait_all(gather4, send_sems.at[3], SAME_CORE)
-    for n, buffer in enumerate((relay_out1, relay_out3, relay_out4)):
+    for n, buffer in enumerate((relay_out1, relay_out3, relay_out4, relay_out2)):
         wait_one(buffer, relay_send.at[n])
     for turn in (0, 1):
         wait_one(rim_in.at[turn], rim_send.at[turn])
-    store_c.wait()
 
 
 def level_scratch(count):
@@ -793,9 +796,11 @@
             *[pltpu.VMEM(shape, F32) for shape in ((32, 32, 128),) * 2 + ((32, 1024),) * 2 + ((2, 32, 1024),) * 2],
             *[pltpu.SMEM(shape, jnp.int32) for shape in (tables[0].shape, tables[1].shape, (2, 16), (3, 2, 16))],
             pltpu.VMEM((8, 2, 32, 128), F32),
-            pltpu.VMEM((16, 32, 128), F32),
+            pltpu.VMEM((8, 32, 128), F32),
             pltpu.VMEM((8, 56, 128), F32),
             pltpu.VMEM((8, 56, 128), F32),
+            pltpu.VMEM((32, 128), F32),
+            pltpu.VMEM((32, 128), F32),
             pltpu.VMEM((32, 128), F32),
             pltpu.VMEM((32, 128), F32),
             pltpu.VMEM((56, 128), F32),
@@ -827,12 +832,11 @@
             *level_scratch(1),
             pltpu.SemaphoreType.DMA((4,)),
             pltpu.SemaphoreType.DMA((4,)),
-            pltpu.SemaphoreType.DMA((3,)),
-            pltpu.SemaphoreType.DMA((3,)),
+            pltpu.SemaphoreType.DMA((4,)),
+            pltpu.SemaphoreType.DMA((4,)),
             pltpu.SemaphoreType.DMA((2,)),
             pltpu.SemaphoreType.DMA((6,)),
             pltpu.SemaphoreType.DMA((10,)),
-            pltpu.SemaphoreType.DMA,
         ],
         compiler_params=pltpu.CompilerParams(
             collective_id=0, has_side_effects=True, vmem_limit_bytes=40 * 2**20

time: 47.5 us -> 46 us (0.968)
  Pallas kernels: 46.8 us -> 45.2 us
    pallas_call x2, Pallas kernels: 46.8 us -> 45.2 us  [on_device(): return tuple(write(*call(*pinned)))]
where the time goes in v3:
time: 46 us; the launch traced here: 45.8 us
  Pallas kernels  45.2 us (98%)
  between operations  0.64 us (1%)
    pallas_call x2, Pallas kernels, on_device(): return tuple(write(*call(*pinned)))  45.2 us

profile of v3, /device:TPU:1, one launch (start us, length us, event | category | flops | bytes accessed | tf_op | source)
XLA Modules:
  0.0 45.8 jit_solution(2721718179719221563)
XLA Ops:
  0.6 44.2 %v_cycle.1 = (f32[32,32,128]{2,1,0:T(8,128)S(1)}, f32[1,1,32,1024]{3,2,1,0:T(8,128)S(1)}, f32[1,1,2,32,1024]{4,3,2,1,0:T(8,128)S(1)}) custom-call(f32[32,32,128]{2,1,0:T(8,128)} %far_rhs_c.1, f32[32,32,128]{2,1,0:T(8,128)} %far_beta_c.1, f32[1,1,32,1024]{3,2,1,0:T(8,128)} %far_rhs_m.1, f32[1,1,32,1024]{3,2,1,0:T(8,128)} %far_beta_m.1, ...), custom_call_target="tpu_custom_call" | custom-call | tf_op jit(solution)/shard_map/v_cycle/pallas_call | solution.py:856
  44.9 0.9 %write_out.1 = (f32[32,32,128]{2,1,0:T(8,128)}, f32[1,1,32,1024]{3,2,1,0:T(8,128)}, f32[1,1,2,32,1024]{4,3,2,1,0:T(8,128)}) custom-call(f32[32,32,128]{2,1,0:T(8,128)S(1)} %get-tuple-element.6.refs_0_, f32[1,1,32,1024]{3,2,1,0:T(8,128)S(1)} %get-tuple-element.7.refs_1_, f32[1,1,2,32,1024]{4,3,2,1,0:T(8,128)S(1)} %get-tuple-element.8.refs_2_), custom_call_target="tpu_custom_call" | custom-call | tf_op jit(solution)/shard_map/write_out/pallas_call | solution.py:856

commit v4 on v3

--- a/solution.py
+++ b/solution.py
@@ -17,7 +17,6 @@
 WIDE = 2 * EDGE + PAIRS * ROWS
 CHIPS = ((2, 1), (1, 1), (3, 1), (2, 0), (0, 1), (1, 0), (3, 0))
 SAME_CORE = [(dx, dh, 0) for dx, dh in CHIPS]
-PEERS = [(dx, dh, dc) for dx, dh in CHIPS for dc in (0, 1)] + [(0, 0, 1)]
 
 
 def iota(shape, dim):
@@ -320,7 +319,8 @@
         return (((x + dx) % 4) * 4 + ((h + dh) % 2) * 2 + (c + dc) % 2, col)
 
     barrier = pltpu.get_barrier_semaphore()
-    greeted = [peer(*hop) for hop in PEERS] + [beside(dx, dy) for dx in (-1, 0, 1) for dy in (-1, 1)]
+    greeted = [peer(*hop) for hop in SAME_CORE] + [peer(0, 0, 1), beside(-1, 0), beside(1, 0)]
+    greeted += [beside(dx, dy) for dx in (-1, 0, 1) for dy in (-1, 1)]
     for device in greeted:
         pl.semaphore_signal(barrier, inc=1, device_id=device, device_id_type=MESH)
 

time: 46 us -> 45.7 us (level)
  no operation moved by 1% of the time
where the time goes in v4:
time: 45.7 us; the launch traced here: 45.6 us
  Pallas kernels  44.9 us (98%)
  between operations  0.64 us (1%)
    pallas_call x2, Pallas kernels, on_device(): return tuple(write(*call(*pinned)))  44.9 us

profile of v4, /device:TPU:1, one launch (start us, length us, event | category | flops | bytes accessed | tf_op | source)
XLA Modules:
  0.0 45.6 jit_solution(17038147549336037732)
XLA Ops:
  0.6 44.0 %v_cycle.1 = (f32[32,32,128]{2,1,0:T(8,128)S(1)}, f32[1,1,32,1024]{3,2,1,0:T(8,128)S(1)}, f32[1,1,2,32,1024]{4,3,2,1,0:T(8,128)S(1)}) custom-call(f32[32,32,128]{2,1,0:T(8,128)} %far_rhs_c.1, f32[32,32,128]{2,1,0:T(8,128)} %far_beta_c.1, f32[1,1,32,1024]{3,2,1,0:T(8,128)} %far_rhs_m.1, f32[1,1,32,1024]{3,2,1,0:T(8,128)} %far_beta_m.1, ...), custom_call_target="tpu_custom_call" | custom-call | tf_op jit(solution)/shard_map/v_cycle/pallas_call | solution.py:856
  44.6 0.9 %write_out.1 = (f32[32,32,128]{2,1,0:T(8,128)}, f32[1,1,32,1024]{3,2,1,0:T(8,128)}, f32[1,1,2,32,1024]{4,3,2,1,0:T(8,128)}) custom-call(f32[32,32,128]{2,1,0:T(8,128)S(1)} %get-tuple-element.6.refs_0_, f32[1,1,32,1024]{3,2,1,0:T(8,128)S(1)} %get-tuple-element.7.refs_1_, f32[1,1,2,32,1024]{4,3,2,1,0:T(8,128)S(1)} %get-tuple-element.8.refs_2_), custom_call_target="tpu_custom_call" | custom-call | tf_op jit(solution)/shard_map/write_out/pallas_call | solution.py:856

commit v5 on v4

--- a/solution.py
+++ b/solution.py
@@ -15,7 +15,7 @@
 ROWS = 48
 EDGE = 56
 WIDE = 2 * EDGE + PAIRS * ROWS
-CHIPS = ((2, 1), (1, 1), (3, 1), (2, 0), (0, 1), (1, 0), (3, 0))
+CHIPS = ((2, 1), (1, 1), (3, 1), (0, 1), (2, 0), (1, 0), (3, 0))
 SAME_CORE = [(dx, dh, 0) for dx, dh in CHIPS]
 
 

time: 45.7 us -> 45.7 us (level)
  no operation moved by 1% of the time
where the time goes in v5:
time: 45.7 us; the launch traced here: 45.6 us
  Pallas kernels  44.9 us (98%)
  between operations  0.64 us (1%)
    pallas_call x2, Pallas kernels, on_device(): return tuple(write(*call(*pinned)))  44.9 us

profile of v5, /device:TPU:1, one launch (start us, length us, event | category | flops | bytes accessed | tf_op | source)
XLA Modules:
  0.0 45.6 jit_solution(763793654425152897)
XLA Ops:
  0.6 44.0 %v_cycle.1 = (f32[32,32,128]{2,1,0:T(8,128)S(1)}, f32[1,1,32,1024]{3,2,1,0:T(8,128)S(1)}, f32[1,1,2,32,1024]{4,3,2,1,0:T(8,128)S(1)}) custom-call(f32[32,32,128]{2,1,0:T(8,128)} %far_rhs_c.1, f32[32,32,128]{2,1,0:T(8,128)} %far_beta_c.1, f32[1,1,32,1024]{3,2,1,0:T(8,128)} %far_rhs_m.1, f32[1,1,32,1024]{3,2,1,0:T(8,128)} %far_beta_m.1, ...), custom_call_target="tpu_custom_call" | custom-call | tf_op jit(solution)/shard_map/v_cycle/pallas_call | solution.py:856
  44.6 0.9 %write_out.1 = (f32[32,32,128]{2,1,0:T(8,128)}, f32[1,1,32,1024]{3,2,1,0:T(8,128)}, f32[1,1,2,32,1024]{4,3,2,1,0:T(8,128)}) custom-call(f32[32,32,128]{2,1,0:T(8,128)S(1)} %get-tuple-element.6.refs_0_, f32[1,1,32,1024]{3,2,1,0:T(8,128)S(1)} %get-tuple-element.7.refs_1_, f32[1,1,2,32,1024]{4,3,2,1,0:T(8,128)S(1)} %get-tuple-element.8.refs_2_), custom_call_target="tpu_custom_call" | custom-call | tf_op jit(solution)/shard_map/write_out/pallas_call | solution.py:856
